TPU v7x, 32 devices: a whole 2x2x4 slice. The times are simulated.
32 devices in a mesh: dp: 4 (over x, core), row: 2 (over y), col: 4 (over z).
Axes of the slice: x: 2, y: 2, z: 4, core: 2. Of those that a mesh axis runs over, the one named last changes fastest.
Arguments:
- layer_input: bfloat16 [32768, 1024], P(('dp', 'row', 'col')), may hold values from -6 to 6
- segment_ids: int32 [32, 1024], P(('dp', 'row', 'col')), may hold values from 0 to 7, never falling along the last dimension, each value on 1 to 512 neighbouring positions
- norm1_gain: bfloat16 [1024], P(('row', 'col')), may hold values from 0.5 to 1.5
- query_weight: bfloat16 [1024, 512], P('row', 'col')
- key_weight: bfloat16 [1024, 512], P('row', 'col')
- value_weight: bfloat16 [1024, 1024], P('row', 'col'), may hold values from -0.1875 to 0.1875
- outgate_weight: bfloat16 [1024, 1024], P('row', 'col'), may hold values from -0.1875 to 0.1875
- decay_down: bfloat16 [1024, 16], P('row', 'col'), may hold values from -0.1875 to 0.1875
- decay_up: bfloat16 [16, 512], P('row', 'col'), may hold values from -1.5 to 1.5
- decay_bias: bfloat16 [512], P(('row', 'col')), may hold values from -1 to 4
- head_gain: bfloat16 [256], P(('row', 'col')), may hold values from 0.5 to 1.5
- out_weight: bfloat16 [1024, 1024], P('row', 'col'), may hold values from -0.375 to 0.375
- norm2_gain: bfloat16 [1024], P(('row', 'col')), may hold values from 0.5 to 1.5
- swiglu_gate: bfloat16 [1024, 2816], P('row', 'col'), may hold values from -0.1875 to 0.1875
- swiglu_up: bfloat16 [1024, 2816], P('row', 'col'), may hold values from -0.1875 to 0.1875
- swiglu_down: bfloat16 [2816, 1024], P('row', 'col'), may hold values from -0.109375 to 0.109375
- cotangent: bfloat16 [32768, 1024], P(('dp', 'row', 'col')), may hold values from -6 to 6
Outputs:
- layer_output: bfloat16 [32768, 1024], P(('dp', 'row', 'col'))
- input_grad: float32 [32768, 1024], P(('dp', 'row', 'col'))
- grad_norm1_gain: float32 [1024], P(('row', 'col'))
- grad_query_weight: float32 [1024, 512], P('row', 'col')
- grad_key_weight: float32 [1024, 512], P('row', 'col')
- grad_value_weight: float32 [1024, 1024], P('row', 'col')
- grad_outgate_weight: float32 [1024, 1024], P('row', 'col')
- grad_decay_down: float32 [1024, 16], P('row', 'col')
- grad_decay_up: float32 [16, 512], P('row', 'col')
- grad_decay_bias: float32 [512], P(('row', 'col'))
- grad_head_gain: float32 [256], P(('row', 'col'))
- grad_out_weight: float32 [1024, 1024], P('row', 'col')
- grad_norm2_gain: float32 [1024], P(('row', 'col'))
- grad_swiglu_gate: float32 [1024, 2816], P('row', 'col')
- grad_swiglu_up: float32 [1024, 2816], P('row', 'col')
- grad_swiglu_down: float32 [2816, 1024], P('row', 'col')
Inputs may be any that keep to these rules, and one draw needn't show every extreme that they name: `segment_ids`: within each packed row the ids never fall; a document covers at most 512 positions and one covers exactly that many; every row holds all eight ids.
All inputs are finite; a program needn't handle non-finite values.
Results may differ from a plain program's by a relative error of at most 0.02.
Values may be sent and summed in bfloat16 or wider, within the bound.
No kernel may reach another device: no remote copies, remote signals or barrier semaphores. Data moves between devices by JAX's collectives and lax.ppermute only.
A program may use at most 320 MiB of HBM per device.

v0:
```python
import jax
import jax.numpy as jnp
from jax import lax
from jax.sharding import PartitionSpec as P

HEADS = 4
HK = 128
HV = 256
CH = 64


EPS = 1e-05
HIGH = lax.Precision.HIGHEST


def unpack(initials, gathered, row_count, col_count):
    result = []
    for initial, member in zip(initials, gathered):
        if initial.ndim == 2:
            row_size = initial.shape[0]
            col_size = initial.shape[1]
            blocked = member.reshape(row_count, col_count, row_size, col_size).transpose(0, 2, 1, 3)
            result.append(blocked.reshape(row_count * row_size, col_count * col_size))
        else:
            result.append(member.reshape(-1))
    return result


def grid_blocks(full, row_count, col_count):
    if full.ndim == 1:
        return full.reshape(row_count * col_count, -1)
    row_size = full.shape[0] // row_count
    col_size = full.shape[1] // col_count
    blocked = full.reshape(row_count, row_size, col_count, col_size).transpose(0, 2, 1, 3)
    return blocked.reshape(row_count * col_count, row_size * col_size)


def matmul(left, right):
    return jnp.dot(left, right, preferred_element_type=jnp.float32)


def back_matmul(left, right):
    return jnp.einsum("tq,pq->tp", left, right, preferred_element_type=jnp.float32)


def weight_grad(left, right):
    return jnp.einsum("tp,tq->pq", left, right, preferred_element_type=jnp.float32)


def norm_grad(grad_out, values, inverse, gain):
    scaled = grad_out * gain
    mean_term = jnp.mean(scaled * values, axis=-1, keepdims=True)
    return inverse * (scaled - values * inverse * inverse * mean_term)


def to_spans(array, seq_local, heads, width):
    spans = array.shape[0] // (seq_local * CH)
    return array.reshape(seq_local, spans, CH, heads, width).transpose(1, 0, 2, 3, 4)


def from_spans(array):
    shaped = array.transpose(1, 0, 2, 3, 4)
    return shaped.reshape(
        shaped.shape[0] * shaped.shape[1] * shaped.shape[2], shaped.shape[3] * shaped.shape[4]
    )


def previous_docs(segment_ids):
    seq_local = segment_ids.shape[0]
    span_docs = segment_ids.reshape(seq_local, -1, CH)
    finals = span_docs[:, :, CH - 1]
    before = jnp.concatenate([jnp.full((seq_local, 1), -1, jnp.int32), finals[:, :-1]], axis=1)
    return (span_docs.transpose(1, 0, 2), before.transpose(1, 0))


def span_terms(query_part, key_part, decay_part, doc_part, prev_part):
    cumul = jnp.cumsum(decay_part, axis=1)
    places = jnp.arange(CH, dtype=jnp.int32)
    allowed = (places[:, None] >= places[None, :])[None] & (
        doc_part[:, :, None] == doc_part[:, None, :]
    )
    pair_mask = allowed.astype(jnp.float32)[:, None]
    centre = cumul[:, CH // 2 - 1 : CH // 2]
    rise = jnp.exp(cumul - centre)
    fall = jnp.exp(centre - cumul)
    query_scaled = query_part * rise
    key_scaled = key_part * fall
    last_doc = doc_part[:, CH - 1]
    enter = (doc_part == prev_part[:, None]).astype(jnp.float32)[:, :, None, None]
    carry_on = (last_doc == prev_part).astype(jnp.float32)[:, None, None, None]
    same_doc = (doc_part == last_doc[:, None]).astype(jnp.float32)[:, :, None, None]
    growth = jnp.exp(cumul)
    to_end = jnp.exp(cumul[:, CH - 1 :] - cumul)
    return (
        pair_mask,
        query_scaled,
        key_scaled,
        rise,
        fall,
        enter,
        carry_on,
        same_doc,
        growth,
        to_end,
    )


def attend_forward(query, keys, values, log_decay, segment_ids):
    seq_local = segment_ids.shape[0]
    key_scale = HK ** (-0.5)
    query_c = to_spans(query.astype(jnp.float32), seq_local, HEADS, HK)
    key_c = to_spans(keys.astype(jnp.float32), seq_local, HEADS, HK)
    value_c = to_spans(values.astype(jnp.float32), seq_local, HEADS, HV)
    decay_c = to_spans(log_decay, seq_local, HEADS, HK)
    doc_spans, prev_docs = previous_docs(segment_ids)

    def step(carried, inputs):
        query_part, key_part, value_part, decay_part, doc_part, prev_part = inputs
        (
            pair_mask,
            query_scaled,
            key_scaled,
            rise,
            fall,
            enter,
            carry_on,
            same_doc,
            growth,
            to_end,
        ) = span_terms(query_part, key_part, decay_part, doc_part, prev_part)
        scores = jnp.einsum("athi,ashi->ahts", query_scaled, key_scaled, precision=HIGH) * (
            key_scale * pair_mask
        )
        local_out = jnp.einsum("ahts,ashj->athj", scores, value_part, precision=HIGH)
        carried_out = (
            jnp.einsum("athi,ahij->athj", query_part * growth * enter, carried, precision=HIGH)
            * key_scale
        )
        next_state = carry_on * growth[:, CH - 1][..., None] * carried + jnp.einsum(
            "ashi,ashj->ahij", key_part * to_end * same_doc, value_part, precision=HIGH
        )
        return (next_state, (local_out + carried_out, carried))

    start = jnp.zeros((seq_local, HEADS, HK, HV), jnp.float32)
    final_state, results = lax.scan(
        step, start, (query_c, key_c, value_c, decay_c, doc_spans, prev_docs)
    )
    outputs, states = results
    return (from_spans(outputs), states)


def attend_backward(query, keys, values, log_decay, segment_ids, states, grad_mixed):
    seq_local = segment_ids.shape[0]
    key_scale = HK ** (-0.5)
    query_c = to_spans(query.astype(jnp.float32), seq_local, HEADS, HK)
    key_c = to_spans(keys.astype(jnp.float32), seq_local, HEADS, HK)
    value_c = to_spans(values.astype(jnp.float32), seq_local, HEADS, HV)
    decay_c = to_spans(log_decay, seq_local, HEADS, HK)
    grad_c = to_spans(grad_mixed, seq_local, HEADS, HV)
    doc_spans, prev_docs = previous_docs(segment_ids)

    def step(grad_state, inputs):
        query_part, key_part, value_part, decay_part, doc_part, prev_part, state_part, grad_part = (
            inputs
        )
        (
            pair_mask,
            query_scaled,
            key_scaled,
            rise,
            fall,
            enter,
            carry_on,
            same_doc,
            growth,
            to_end,
        ) = span_terms(query_part, key_part, decay_part, doc_part, prev_part)
        scores = jnp.einsum("athi,ashi->ahts", query_scaled, key_scaled, precision=HIGH) * (
            key_scale * pair_mask
        )
        grad_scores = jnp.einsum("athj,ashj->ahts", grad_part, value_part, precision=HIGH) * (
            key_scale * pair_mask
        )
        weighted_keys = key_part * to_end * same_doc
        grad_value = jnp.einsum("ahts,athj->ashj", scores, grad_part, precision=HIGH) + jnp.einsum(
            "ashi,ahij->ashj", weighted_keys, grad_state, precision=HIGH
        )
        grad_weighted = (
            jnp.einsum("ahij,ashj->ashi", grad_state, value_part, precision=HIGH) * same_doc
        )
        grad_growth = (
            jnp.einsum("athj,ahij->athi", grad_part, state_part, precision=HIGH) * key_scale * enter
        )
        query_inner = jnp.einsum("ahts,ashi->athi", grad_scores, key_scaled, precision=HIGH) * rise
        key_inner = jnp.einsum("ahts,athi->ashi", grad_scores, query_scaled, precision=HIGH) * fall
        grad_query = query_inner + grad_growth * growth
        grad_key = key_inner + grad_weighted * to_end
        end_terms = grad_weighted * key_part * to_end
        grad_cumul = (
            query_part * query_inner
            - key_part * key_inner
            + grad_growth * query_part * growth
            - end_terms
        )
        last_grad = (
            jnp.sum(end_terms, axis=1)
            + carry_on[:, 0]
            * jnp.einsum("ahij,ahij->ahi", grad_state, state_part, precision=HIGH)
            * growth[:, CH - 1]
        )
        grad_cumul = grad_cumul.at[:, CH - 1].add(last_grad)
        grad_decay = lax.cumsum(grad_cumul, axis=1, reverse=True)
        grad_prev = (
            carry_on * growth[:, CH - 1][..., None] * grad_state
            + jnp.einsum("athi,athj->ahij", query_part * growth * enter, grad_part, precision=HIGH)
            * key_scale
        )
        return (grad_prev, (grad_query, grad_key, grad_value, grad_decay))

    start = jnp.zeros((seq_local, HEADS, HK, HV), jnp.float32)
    first_grad, results = lax.scan(
        step,
        start,
        (query_c, key_c, value_c, decay_c, doc_spans, prev_docs, states, grad_c),
        reverse=True,
    )
    grad_query, grad_key, grad_value, grad_decay = results
    return (
        from_spans(grad_query),
        from_spans(grad_key),
        from_spans(grad_value),
        from_spans(grad_decay),
    )


def per_device(
    layer_input,
    segment_ids,
    norm1_gain,
    query_weight,
    key_weight,
    value_weight,
    outgate_weight,
    decay_down,
    decay_up,
    decay_bias,
    head_gain,
    out_weight,
    norm2_gain,
    swiglu_gate,
    swiglu_up,
    swiglu_down,
    cotangent,
):
    row_count = lax.axis_size("row")
    col_count = lax.axis_size("col")
    attention_own = (
        norm1_gain,
        query_weight,
        key_weight,
        value_weight,
        outgate_weight,
        decay_down,
        decay_up,
        decay_bias,
        head_gain,
        out_weight,
    )
    feedforward_own = (norm2_gain, swiglu_gate, swiglu_up, swiglu_down)
    gathered = (
        lax.all_gather(norm1_gain.reshape(1, -1), ("row", "col"), axis=0, tiled=True),
        lax.all_gather(query_weight.reshape(1, -1), ("row", "col"), axis=0, tiled=True),
        lax.all_gather(key_weight.reshape(1, -1), ("row", "col"), axis=0, tiled=True),
        lax.all_gather(value_weight.reshape(1, -1), ("row", "col"), axis=0, tiled=True),
        lax.all_gather(outgate_weight.reshape(1, -1), ("row", "col"), axis=0, tiled=True),
        lax.all_gather(decay_down.reshape(1, -1), ("row", "col"), axis=0, tiled=True),
        lax.all_gather(decay_up.reshape(1, -1), ("row", "col"), axis=0, tiled=True),
        lax.all_gather(decay_bias.reshape(1, -1), ("row", "col"), axis=0, tiled=True),
        lax.all_gather(head_gain.reshape(1, -1), ("row", "col"), axis=0, tiled=True),
        lax.all_gather(out_weight.reshape(1, -1), ("row", "col"), axis=0, tiled=True),
    )
    attention_full = unpack(attention_own, gathered, row_count, col_count)
    gathered_second = (
        lax.all_gather(norm2_gain.reshape(1, -1), ("row", "col"), axis=0, tiled=True),
        lax.all_gather(swiglu_gate.reshape(1, -1), ("row", "col"), axis=0, tiled=True),
        lax.all_gather(swiglu_up.reshape(1, -1), ("row", "col"), axis=0, tiled=True),
        lax.all_gather(swiglu_down.reshape(1, -1), ("row", "col"), axis=0, tiled=True),
    )
    feedforward_full = unpack(feedforward_own, gathered_second, row_count, col_count)
    (
        gain_one,
        query_full,
        key_full,
        value_full,
        outgate_full,
        down_full,
        decay_up_full,
        bias_full,
        head_full,
        output_full,
    ) = attention_full
    gain_two, gate_full, lift_full, lower_full = feedforward_full
    input_f = layer_input.astype(jnp.float32)
    tokens = input_f.shape[0]
    inv_one = lax.rsqrt(jnp.mean(input_f * input_f, axis=-1, keepdims=True) + EPS)
    normed_one = (input_f * inv_one * gain_one.astype(jnp.float32)).astype(jnp.bfloat16)
    query = matmul(normed_one, query_full).astype(jnp.bfloat16)
    keys = matmul(normed_one, key_full).astype(jnp.bfloat16)
    values = matmul(normed_one, value_full).astype(jnp.bfloat16)
    outgate = matmul(normed_one, outgate_full)
    low_rank = matmul(normed_one, down_full)
    decay_logit = jnp.dot(
        low_rank, decay_up_full.astype(jnp.float32), precision=HIGH
    ) + bias_full.astype(jnp.float32)
    log_decay = jax.nn.log_sigmoid(decay_logit) / 16.0
    mixed, states = attend_forward(query, keys, values, log_decay, segment_ids)
    mixed_heads = mixed.reshape(tokens, HEADS, HV)
    inv_head = lax.rsqrt(jnp.mean(mixed_heads * mixed_heads, axis=-1, keepdims=True) + EPS)
    head_normed = mixed_heads * inv_head * head_full.astype(jnp.float32)
    outgate_heads = outgate.reshape(tokens, HEADS, HV)
    outgate_sig = jax.nn.sigmoid(outgate_heads)
    swish = outgate_heads * outgate_sig
    gated = (head_normed * swish).reshape(tokens, HEADS * HV).astype(jnp.bfloat16)
    middle = input_f + matmul(gated, output_full)
    inv_two = lax.rsqrt(jnp.mean(middle * middle, axis=-1, keepdims=True) + EPS)
    normed_two = (middle * inv_two * gain_two.astype(jnp.float32)).astype(jnp.bfloat16)
    gate_pre = matmul(normed_two, gate_full)
    lift_pre = matmul(normed_two, lift_full)
    gate_sig = jax.nn.sigmoid(gate_pre)
    hidden = (gate_pre * gate_sig * lift_pre).astype(jnp.bfloat16)
    layer_output = (middle + matmul(hidden, lower_full)).astype(jnp.bfloat16)
    regathered = (
        lax.all_gather(norm1_gain.reshape(1, -1), ("row", "col"), axis=0, tiled=True),
        lax.all_gather(query_weight.reshape(1, -1), ("row", "col"), axis=0, tiled=True),
        lax.all_gather(key_weight.reshape(1, -1), ("row", "col"), axis=0, tiled=True),
        lax.all_gather(value_weight.reshape(1, -1), ("row", "col"), axis=0, tiled=True),
        lax.all_gather(outgate_weight.reshape(1, -1), ("row", "col"), axis=0, tiled=True),
        lax.all_gather(decay_down.reshape(1, -1), ("row", "col"), axis=0, tiled=True),
        lax.all_gather(decay_up.reshape(1, -1), ("row", "col"), axis=0, tiled=True),
        lax.all_gather(decay_bias.reshape(1, -1), ("row", "col"), axis=0, tiled=True),
        lax.all_gather(head_gain.reshape(1, -1), ("row", "col"), axis=0, tiled=True),
        lax.all_gather(out_weight.reshape(1, -1), ("row", "col"), axis=0, tiled=True),
    )
    attention_back = unpack(attention_own, regathered, row_count, col_count)
    regathered_second = (
        lax.all_gather(norm2_gain.reshape(1, -1), ("row", "col"), axis=0, tiled=True),
        lax.all_gather(swiglu_gate.reshape(1, -1), ("row", "col"), axis=0, tiled=True),
        lax.all_gather(swiglu_up.reshape(1, -1), ("row", "col"), axis=0, tiled=True),
        lax.all_gather(swiglu_down.reshape(1, -1), ("row", "col"), axis=0, tiled=True),
    )
    feedforward_back = unpack(feedforward_own, regathered_second, row_count, col_count)
    (
        back_gain_one,
        back_query,
        back_key,
        back_value,
        back_outgate,
        back_down,
        back_decay_up,
        unused_bias,
        back_head,
        back_output,
    ) = attention_back
    back_gain_two, back_gate, back_lift, back_lower = feedforward_back
    gain_one_f = back_gain_one.astype(jnp.float32)
    gain_two_f = back_gain_two.astype(jnp.float32)
    head_gain_f = back_head.astype(jnp.float32)
    decay_up_f = back_decay_up.astype(jnp.float32)
    grad_top = cotangent.astype(jnp.float32)
    grad_lower_w = weight_grad(hidden, cotangent)
    grad_hidden = back_matmul(cotangent, back_lower)
    grad_lift = (grad_hidden * gate_pre * gate_sig).astype(jnp.bfloat16)
    grad_gate = (grad_hidden * lift_pre * gate_sig * (1.0 + gate_pre * (1.0 - gate_sig))).astype(
        jnp.bfloat16
    )
    grad_gate_w = weight_grad(normed_two, grad_gate)
    grad_lift_w = weight_grad(normed_two, grad_lift)
    grad_normed_two = back_matmul(grad_gate, back_gate) + back_matmul(grad_lift, back_lift)
    grad_gain_two = jnp.sum(grad_normed_two * middle * inv_two, axis=0)
    grad_middle = grad_top + norm_grad(grad_normed_two, middle, inv_two, gain_two_f)
    grad_branch = grad_middle.astype(jnp.bfloat16)
    grad_output_w = weight_grad(gated, grad_branch)
    grad_gated = back_matmul(grad_branch, back_output).reshape(tokens, HEADS, HV)
    grad_outgate = (
        grad_gated * head_normed * outgate_sig * (1.0 + outgate_heads * (1.0 - outgate_sig))
    )
    grad_outgate = grad_outgate.reshape(tokens, HEADS * HV).astype(jnp.bfloat16)
    grad_head_normed = grad_gated * swish
    grad_head_gain = jnp.sum(grad_head_normed * mixed_heads * inv_head, axis=(0, 1))
    grad_mixed = norm_grad(grad_head_normed, mixed_heads, inv_head, head_gain_f).reshape(
        tokens, HEADS * HV
    )
    grad_query, grad_key, grad_value, grad_log = attend_backward(
        query, keys, values, log_decay, segment_ids, states, grad_mixed
    )
    grad_logit = grad_log / 16.0 * jax.nn.sigmoid(-decay_logit)
    grad_bias = jnp.sum(grad_logit, axis=0)
    grad_decay_up = jnp.einsum("tl,tk->lk", low_rank, grad_logit, precision=HIGH)
    grad_low = jnp.einsum("tk,lk->tl", grad_logit, decay_up_f, precision=HIGH).astype(jnp.bfloat16)
    grad_query_low = grad_query.astype(jnp.bfloat16)
    grad_key_low = grad_key.astype(jnp.bfloat16)
    grad_value_low = grad_value.astype(jnp.bfloat16)
    grad_query_w = weight_grad(normed_one, grad_query_low)
    grad_key_w = weight_grad(normed_one, grad_key_low)
    grad_value_w = weight_grad(normed_one, grad_value_low)
    grad_outgate_w = weight_grad(normed_one, grad_outgate)
    grad_down_w = weight_grad(normed_one, grad_low)
    grad_normed_one = (
        back_matmul(grad_query_low, back_query)
        + back_matmul(grad_key_low, back_key)
        + back_matmul(grad_value_low, back_value)
        + back_matmul(grad_outgate, back_outgate)
        + back_matmul(grad_low, back_down)
    )
    grad_gain_one = jnp.sum(grad_normed_one * input_f * inv_one, axis=0)
    input_grad = grad_middle + norm_grad(grad_normed_one, input_f, inv_one, gain_one_f)
    attention_sums = (
        lax.psum_scatter(
            grid_blocks(grad_gain_one, row_count, col_count),
            ("row", "col"),
            scatter_dimension=0,
            tiled=True,
        ),
        lax.psum_scatter(
            grid_blocks(grad_query_w, row_count, col_count),
            ("row", "col"),
            scatter_dimension=0,
            tiled=True,
        ),
        lax.psum_scatter(
            grid_blocks(grad_key_w, row_count, col_count),
            ("row", "col"),
            scatter_dimension=0,
            tiled=True,
        ),
        lax.psum_scatter(
            grid_blocks(grad_value_w, row_count, col_count),
            ("row", "col"),
            scatter_dimension=0,
            tiled=True,
        ),
        lax.psum_scatter(
            grid_blocks(grad_outgate_w, row_count, col_count),
            ("row", "col"),
            scatter_dimension=0,
            tiled=True,
        ),
        lax.psum_scatter(
            grid_blocks(grad_down_w, row_count, col_count),
            ("row", "col"),
            scatter_dimension=0,
            tiled=True,
        ),
        lax.psum_scatter(
            grid_blocks(grad_decay_up, row_count, col_count),
            ("row", "col"),
            scatter_dimension=0,
            tiled=True,
        ),
        lax.psum_scatter(
            grid_blocks(grad_bias, row_count, col_count),
            ("row", "col"),
            scatter_dimension=0,
            tiled=True,
        ),
        lax.psum_scatter(
            grid_blocks(grad_head_gain, row_count, col_count),
            ("row", "col"),
            scatter_dimension=0,
            tiled=True,
        ),
        lax.psum_scatter(
            grid_blocks(grad_output_w, row_count, col_count),
            ("row", "col"),
            scatter_dimension=0,
            tiled=True,
        ),
    )
    feedforward_sums = (
        lax.psum_scatter(
            grid_blocks(grad_gain_two, row_count, col_count),
            ("row", "col"),
            scatter_dimension=0,
            tiled=True,
        ),
        lax.psum_scatter(
            grid_blocks(grad_gate_w, row_count, col_count),
            ("row", "col"),
            scatter_dimension=0,
            tiled=True,
        ),
        lax.psum_scatter(
            grid_blocks(grad_lift_w, row_count, col_count),
            ("row", "col"),
            scatter_dimension=0,
            tiled=True,
        ),
        lax.psum_scatter(
            grid_blocks(grad_lower_w, row_count, col_count),
            ("row", "col"),
            scatter_dimension=0,
            tiled=True,
        ),
    )
    totals = (
        lax.psum(attention_sums[0].astype(jnp.bfloat16), "dp").astype(jnp.float32),
        lax.psum(attention_sums[1].astype(jnp.bfloat16), "dp").astype(jnp.float32),
        lax.psum(attention_sums[2].astype(jnp.bfloat16), "dp").astype(jnp.float32),
        lax.psum(attention_sums[3].astype(jnp.bfloat16), "dp").astype(jnp.float32),
        lax.psum(attention_sums[4].astype(jnp.bfloat16), "dp").astype(jnp.float32),
        lax.psum(attention_sums[5].astype(jnp.bfloat16), "dp").astype(jnp.float32),
        lax.psum(attention_sums[6].astype(jnp.bfloat16), "dp").astype(jnp.float32),
        lax.psum(attention_sums[7].astype(jnp.bfloat16), "dp").astype(jnp.float32),
        lax.psum(attention_sums[8].astype(jnp.bfloat16), "dp").astype(jnp.float32),
        lax.psum(attention_sums[9].astype(jnp.bfloat16), "dp").astype(jnp.float32),
        lax.psum(feedforward_sums[0].astype(jnp.bfloat16), "dp").astype(jnp.float32),
        lax.psum(feedforward_sums[1].astype(jnp.bfloat16), "dp").astype(jnp.float32),
        lax.psum(feedforward_sums[2].astype(jnp.bfloat16), "dp").astype(jnp.float32),
        lax.psum(feedforward_sums[3].astype(jnp.bfloat16), "dp").astype(jnp.float32),
    )
    owners = attention_own + feedforward_own
    shaped = [total.reshape(owner.shape) for total, owner in zip(totals, owners)]
    return (
        layer_output,
        input_grad,
        shaped[0],
        shaped[1],
        shaped[2],
        shaped[3],
        shaped[4],
        shaped[5],
        shaped[6],
        shaped[7],
        shaped[8],
        shaped[9],
        shaped[10],
        shaped[11],
        shaped[12],
        shaped[13],
    )


def solution(mesh):
    in_specs = (
        P(("dp", "row", "col"), None),
        P(("dp", "row", "col"), None),
        P(("row", "col")),
        P("row", "col"),
        P("row", "col"),
        P("row", "col"),
        P("row", "col"),
        P("row", "col"),
        P("row", "col"),
        P(("row", "col")),
        P(("row", "col")),
        P("row", "col"),
        P(("row", "col")),
        P("row", "col"),
        P("row", "col"),
        P("row", "col"),
        P(("dp", "row", "col"), None),
    )
    out_specs = (
        P(("dp", "row", "col"), None),
        P(("dp", "row", "col"), None),
        P(("row", "col")),
        P("row", "col"),
        P("row", "col"),
        P("row", "col"),
        P("row", "col"),
        P("row", "col"),
        P("row", "col"),
        P(("row", "col")),
        P(("row", "col")),
        P("row", "col"),
        P(("row", "col")),
        P("row", "col"),
        P("row", "col"),
        P("row", "col"),
    )
    return jax.shard_map(
        per_device, mesh=mesh, in_specs=in_specs, out_specs=out_specs, check_vma=False
    )
```

profile of v0, /device:TPU:9, one launch (start us, length us, event | category | flops | bytes accessed | tf_op | source)
XLA Modules:
  0.0 3757.0 jit_solution(2554336201482543550)
XLA Ops:
  45.4 23.9 all-gather.5
  75.1 17.1 all-gather.4
  92.7 21.6 all-gather.6
  123.7 15.9 all-gather.12
  220.5 181.2 %while.41 = (s32[]{:T(128)}, f32[1,4,128,256]{3,2,1,0:T(8,128)S(1)}, f32[16,1,64,4,256]{4,2,3,1,0:T(8,128)}, f32[16,1,4,128,256]{4,3,2,1,0:T(8,128)}, s32[16,1,6...) while((s32[]{:T(128)}, ...), condition=%wide.region_3.4_spmd.clone.clone, body=%wide.region_1.3_spmd.clone.sunk.clone | while | flops 280003328 | bytes 5820091 | solution.py:145
  478.0 20.2 all-gather.35.cloned.1.call-done
  498.3 35.9 reduce.26
  553.2 16.5 copy.459
  576.7 86.1 %all-gather.37.cloned.1.call-done = bf16[8,1,360448]{2,1,0:T(2,128)(2,1)} async-done(((bf16[1,1,360448]{2,1,0:T(2,128)(2,1)}), bf16[8,1,360448]{2,1,0:T(2,128)(2,1)}) %all-gather.37.cloned.1.call-update) | async-done | bytes 5767184 | tf_op jit(solution)/shard_map/all_gather | solution.py:286
  662.8 35.6 reduce.25
  717.7 16.5 copy.461
  761.4 65.9 %all-gather.39.cloned.1.call-done = bf16[8,1,360448]{2,1,0:T(2,128)(2,1)} async-done(((bf16[1,1,360448]{2,1,0:T(2,128)(2,1)}), bf16[8,1,360448]{2,1,0:T(2,128)(2,1)}) %all-gather.39.cloned.1.call-update) | async-done | bytes 5767184 | tf_op jit(solution)/shard_map/all_gather | solution.py:287
  827.4 36.1 reduce.24
  867.3 22.4 copy.462
  894.2 21.7 multiply_convert_fusion
  981.9 380.7 %while.42 = (s32[]{:T(128)}, f32[1,4,128,256]{3,2,1,0:T(8,128)S(1)}, bf16[16,1,64,4,128]{4,3,2,1,0:T(4,128)(2,1)S(1)}, bf16[16,1,64,4,128]{4,2,3,1,0:T(8,128)(2,...) while((s32[]{:T(128)}, ...), condition=%wide.region_12.13_spmd.clone.clone, body=%wide.region_8.12_spmd.clone.sunk.clone | while | flops 585287552 | bytes 12620048 | solution.py:221
  1425.3 18.9 copy.491
  1485.7 19.3 copy.493
  1613.4 17.1 copy.563
  1630.5 1965.0 %all-reduce.24 = (bf16[8,2048]{1,0:T(8,128)(2,1)}, bf16[8,360448]{1,0:T(8,128)(2,1)}, bf16[8,360448]{1,0:T(8,128)(2,1)}, bf16[8,128]{1,0:T(8,128)(2,1)S(1)}, bf1...) all-reduce(f32[8,2048]{1,0:T(8,128)S(1)} %reshape.1137, ...), channel_id=11, replica_groups=mesh['dp'=4,'row'=2,'col'=4] {'row','col'}, use_global_device_ids=true, to_apply=%region_25.26.clone | all-reduce | flops 12872448 | bytes 77234688
  3595.5 16.4 fusion.129
  3613.5 18.1 fusion.127
  3671.4 24.7 all-reduce.18
  3699.4 37.1 all-reduce.23.cloned.1.call-done
  (1057 shorter events, 1164.4 us)
Async XLA Ops:
  7.2 136.3 %all-gather.25.cloned.1.call-start = ((), (), s32[]{:S(2)}) async-start(), calls=%async_computation | async-start | bytes 2359296 | tf_op jit(solution)/shard_map/all_gather | solution.py:273
  9.0 152.5 %all-gather.29.cloned.1.call-start = ((), (), s32[]{:S(2)}) async-start(), calls=%async_computation.2 | async-start | bytes 2359296 | tf_op jit(solution)/shard_map/all_gather | solution.py:272
  10.7 175.2 %all-gather.27.cloned.1.call-start = ((), (), s32[]{:S(2)}) async-start(), calls=%async_computation.1 | async-start | bytes 4718592 | tf_op jit(solution)/shard_map/all_gather | solution.py:274
  12.6 403.1 %all-gather.31.cloned.1.call-start = ((), (), s32[]{:S(2)}) async-start(), calls=%async_computation.3 | async-start | bytes 4718592 | tf_op jit(solution)/shard_map/all_gather | solution.py:275
  14.6 424.4 %all-gather.33.cloned.1.call-start = ((), (), s32[]{:S(2)}) async-start(), calls=%async_computation.4 | async-start | bytes 4718592 | tf_op jit(solution)/shard_map/all_gather | solution.py:280
  16.5 481.7 %all-gather.35.cloned.1.call-start = ((), (), s32[]{:S(2)}) async-start(), calls=%async_computation.5 | async-start | bytes 12976128 | tf_op jit(solution)/shard_map/all_gather | solution.py:285
  18.9 643.9 %all-gather.37.cloned.1.call-start = ((), (), s32[]{:S(2)}) async-start(), calls=%async_computation.6 | async-start | bytes 12976128 | tf_op jit(solution)/shard_map/all_gather | solution.py:286
  21.3 23.7 copy-start.69
  21.3 806.0 %all-gather.39.cloned.1.call-start = ((), (), s32[]{:S(2)}) async-start(), calls=%async_computation.7 | async-start | bytes 12976128 | tf_op jit(solution)/shard_map/all_gather | solution.py:287
  22.8 3713.7 %all-reduce.23.cloned.1.call-start = ((), (), s32[]{:S(2)}) async-start(), calls=%async_computation.8 | async-start | bytes 6684672 | tf_op jit(solution)/shard_map/psum | solution.py:517
  24.3 50.8 %copy-start.76 = (bf16[128]{0:T(256)(128)(2,1)S(1)}, bf16[128]{0:T(256)(128)(2,1)}, u32[]{:S(2)}) copy-start(bf16[128]{0:T(256)(128)(2,1)} %param.25) | copy-start | bytes 772
  45.0 70.4 %copy-start.67 = (f32[512]{0:T(512)}, f32[512]{0:T(512)S(1)}, u32[]{:S(2)}) copy-start(f32[512]{0:T(512)S(1)} %convert_element_type.296) | copy-start | bytes 6148
  69.5 23.2 copy-start.71
  72.2 42.8 %copy-start.46 = (bf16[2,8,2,512]{3,1,2,0:T(8,128)(2,1)}, bf16[2,8,2,512]{3,1,2,0:T(8,128)(2,1)S(1)}, u32[]{:S(2)}) copy-start(bf16[2,8,2,512]{3,1,2,0:T(8,128)(2,1)S(1)} %copy.537) | copy-start | bytes 98308
  75.1 397.9 %copy-start.1 = (bf16[1024,1024]{0,1:T(8,128)(2,1)}, bf16[1024,1024]{0,1:T(8,128)(2,1)S(1)}, u32[]{:S(2)}) copy-start(bf16[1024,1024]{0,1:T(8,128)(2,1)S(1)} %copy.439) | copy-start | bytes 6291460
  92.2 23.2 copy-start.58
  92.7 28.0 copy-start.60
  123.7 341.1 %copy-start.73 = (f32[256]{0:T(256)}, f32[256]{0:T(256)S(1)}, u32[]{:S(2)}) copy-start(f32[256]{0:T(256)S(1)} %convert_element_type.297) | copy-start | bytes 3076
  139.6 818.1 %copy-start.54 = (f32[8,1,128]{2,1,0:T(1,128)}, f32[8,1,128]{2,1,0:T(1,128)S(1)}, u32[]{:S(2)}) copy-start(f32[8,1,128]{2,1,0:T(1,128)S(1)} %convert_element_type.300) | copy-start | bytes 12292
  415.7 49.1 %copy-start.50 = (f32[1024,4]{0,1:T(4,128)}, f32[1024,4]{0,1:T(4,128)S(1)}, u32[]{:S(2)}) copy-start(f32[1024,4]{0,1:T(4,128)S(1)} %rsqrt.29) | copy-start | bytes 49156
  475.6 482.1 %copy-start.56 = (f32[1024]{0:T(1024)}, f32[1024]{0:T(1024)S(1)}, u32[]{:S(2)}) copy-start(f32[1024]{0:T(1024)S(1)} %add_rsqrt_fusion) | copy-start | bytes 12292
  478.0 274.4 %copy-start.33 = (bf16[1024,1024]{0,1:T(8,128)(2,1)}, bf16[1024,1024]{0,1:T(8,128)(2,1)S(1)}, u32[]{:S(2)}) copy-start(bf16[1024,1024]{0,1:T(8,128)(2,1)S(1)} %multiply_convert_fusion.4) | copy-start | bytes 6291460
  738.7 13.7 copy-start.19
  1613.4 17.1 copy-start.70
  (72 other events, 425.1 us)
Sparse Core Ops, SparseCore 0:
  10.7 50.0 all-gather.24
  63.5 48.3 all-gather.28
  114.6 71.2 all-gather.26
  188.4 71.6 all-gather.30
  262.7 71.6 all-gather.32
  336.9 161.3 all-gather.34
  500.9 161.8 all-gather.36
  665.5 161.8 all-gather.38
  3651.3 85.1 all-reduce.22
where the time goes:
time: 3780 us; the launch traced here: 3760 us
  blocking collectives  2080 us (55%)
  local copies, waits for them, and re-layouts  529 us (14%)
  other arithmetic  480 us (13%)
  matrix products  408 us (11%)
  waiting for transfers between devices  216 us (6%)
    unnamed x2, blocking collectives  1980 us
    unnamed x231, local copies, waits for them, and re-layouts  174 us
    all_gather x1, waiting for transfers between devices, per_device(): lax.all_gather(swiglu_up.reshape(1, -1), ('row', 'col'), axis=0, tiled=True)  86.1 us
  transfers between devices with their start and end apart: 9, of which 5 were waited for; matrix products, arithmetic and copies ran while one was open for 15% of the time, Pallas kernels for 0%

commit v1 on v0

v1 whole, which is shorter than its diff:
```python
import functools

import jax
import jax.numpy as jnp
from jax import lax
from jax.experimental import pallas as pl
from jax.experimental.pallas import tpu as pltpu
from jax.sharding import Mesh
from jax.sharding import PartitionSpec as P

HEADS = 4
HK = 128
HV = 256
CH = 64
LOW = 16
D = 1024
K = HEADS * HK
V = HEADS * HV
FF = 2816
HC = FF // 4
TILE = 256

EPS = 1e-05
HIGH = lax.Precision.HIGHEST
F32 = jnp.float32
BF16 = jnp.bfloat16
AXES = ("x", "core", "row", "col")
MIB = 1024 * 1024


def dot(left, right, precision=None):
    return jnp.dot(left, right, preferred_element_type=F32, precision=precision)


def dot_nt(left, right, precision=None):
    return lax.dot_general(
        left, right, (((1,), (1,)), ((), ())), preferred_element_type=F32, precision=precision
    )


def dot_tn(left, right, precision=None):
    return lax.dot_general(
        left, right, (((0,), (0,)), ((), ())), preferred_element_type=F32, precision=precision
    )


def struct(shape, dtype):
    return jax.ShapeDtypeStruct(shape, dtype)


def fixed(shape):
    return pl.BlockSpec(shape, lambda *i: (0,) * len(shape))


def rows(height, width):
    return pl.BlockSpec((height, width), lambda i: (i, 0))


def cost(flops, moved, trans=0):
    return pl.CostEstimate(flops=int(flops), bytes_accessed=int(moved), transcendentals=int(trans))


def params(mib):
    return pltpu.CompilerParams(vmem_limit_bytes=mib * MIB)


def project_kernel(x_ref, gain_ref, w_ref, ddt_ref, du_ref, bias_ref, n_ref, q_ref, k_ref, v_ref, low_ref, logit_ref):
    x = x_ref[...].astype(F32)
    inverse = lax.rsqrt(jnp.mean(x * x, axis=-1, keepdims=True) + EPS)
    normed = (x * inverse * gain_ref[...]).astype(BF16)
    n_ref[...] = normed
    for c in range(HEADS):
        total = None
        for r in range(2):
            for core in range(2):
                at = r * 512 + core * 256
                part = dot(normed[:, at : at + 256], w_ref[core, r, c])
                total = part if total is None else total + part
        q_ref[:, c * HK : (c + 1) * HK] = total[:, :HK].astype(BF16)
        k_ref[:, c * HK : (c + 1) * HK] = total[:, HK : 2 * HK].astype(BF16)
        v_ref[:, c * HV : (c + 1) * HV] = total[:, 2 * HK :].astype(BF16)
    low = dot_nt(normed[:, :512], ddt_ref[0]) + dot_nt(normed[:, 512:], ddt_ref[1])
    low_ref[...] = low
    logit_ref[...] = dot(low, du_ref[...], HIGH) + bias_ref[...]


def project(x, gain, weights, ddt, du, bias):
    tokens = x.shape[0]
    return pl.pallas_call(
        project_kernel,
        grid=(tokens // TILE,),
        in_specs=[
            rows(TILE, D),
            fixed((1, D)),
            fixed((2, 2, 4, 256, 512)),
            fixed((2, LOW, 512)),
            fixed((LOW, K)),
            fixed((1, K)),
        ],
        out_specs=[rows(TILE, D), rows(TILE, K), rows(TILE, K), rows(TILE, V), rows(TILE, LOW), rows(TILE, K)],
        out_shape=[
            struct((tokens, D), BF16),
            struct((tokens, K), BF16),
            struct((tokens, K), BF16),
            struct((tokens, V), BF16),
            struct((tokens, LOW), F32),
            struct((tokens, K), F32),
        ],
        compiler_params=params(40),
        cost_estimate=cost(2 * tokens * D * 2048, 14 * MIB),
        name="project",
    )(x, gain, weights, ddt, du, bias)


def span_parts(logit, doc_c, doc_r, last_doc, prev_doc):
    lower = lax.broadcasted_iota(jnp.int32, (CH, CH), 0) >= lax.broadcasted_iota(jnp.int32, (CH, CH), 1)
    mask = jnp.where(lower & (doc_c == doc_r), HK ** (-0.5), 0.0)
    log_decay = (jnp.minimum(logit, 0.0) - jnp.log1p(jnp.exp(-jnp.abs(logit)))) * (1.0 / 16.0)
    cumul = dot(lower.astype(F32), log_decay, HIGH)
    centre = cumul[CH // 2 - 1 : CH // 2]
    last = cumul[CH - 1 :]
    rise = jnp.exp(cumul - centre)
    fall = jnp.exp(centre - cumul)
    growth = jnp.exp(cumul)
    to_end = jnp.exp(last - cumul)
    enter = jnp.where(doc_c == prev_doc, HK ** (-0.5), 0.0)
    same = jnp.where(doc_c == last_doc, 1.0, 0.0)
    return mask, rise, fall, growth, to_end, enter, same, jnp.exp(last)


def span_docs(seg_ref, at, first):
    last_doc = seg_ref[at + CH - 1]
    prev_doc = jnp.where(first, -1, seg_ref[jnp.maximum(at - 1, 0)])
    return last_doc, prev_doc


def attend_kernel(spans, seg_ref, q_ref, k_ref, v_ref, logit_ref, dc_ref, dr_ref, mixed_ref, states_ref, state):
    i = pl.program_id(1)
    at = (pl.program_id(0) * spans + i) * CH
    last_doc, prev_doc = span_docs(seg_ref, at, i == 0)

    @pl.when(i == 0)
    def _():
        state[...] = jnp.zeros_like(state)

    mask, rise, fall, growth, to_end, enter, same, keep = span_parts(
        logit_ref[...], dc_ref[...], dr_ref[0], last_doc, prev_doc
    )
    query = q_ref[...].astype(F32)
    keys = k_ref[...].astype(F32)
    qs = (query * rise).astype(BF16)
    ks = (keys * fall).astype(BF16)
    qg = (query * growth * enter).astype(BF16)
    kw = (keys * to_end * same).astype(BF16)
    keep = keep * jnp.where(last_doc == prev_doc, 1.0, 0.0)
    for h in range(HEADS):
        a, b = h * HK, (h + 1) * HK
        va = v_ref[:, h * HV : (h + 1) * HV]
        now = state[h]
        low = now.astype(BF16)
        states_ref[0, h] = low
        scores = (dot_nt(qs[:, a:b], ks[:, a:b]) * mask).astype(BF16)
        mixed_ref[:, h * HV : (h + 1) * HV] = dot(scores, va) + dot_nt(qg[:, a:b], low)
        state[h] = now * keep[:, a:b] + dot_tn(va, kw[:, a:b])


def attend(q, k, v, logit, segs, seg_c, seg_r):
    tokens = q.shape[0]
    seqs = segs.shape[0]
    spans = tokens // seqs // CH

    def part(width):
        return pl.BlockSpec((CH, width), lambda s, i, seg: (s * spans + i, 0))

    return pl.pallas_call(
        functools.partial(attend_kernel, spans),
        grid_spec=pltpu.PrefetchScalarGridSpec(
            num_scalar_prefetch=1,
            grid=(seqs, spans),
            in_specs=[
                part(K),
                part(K),
                part(V),
                part(K),
                part(1),
                pl.BlockSpec((1, 1, CH), lambda s, i, seg: (s * spans + i, 0, 0)),
            ],
            out_specs=[
                part(V),
                pl.BlockSpec((1, HEADS, HV, HK), lambda s, i, seg: (s * spans + i, 0, 0, 0)),
            ],
            scratch_shapes=[pltpu.VMEM((HEADS, HV, HK), F32)],
        ),
        out_shape=[struct((tokens, V), F32), struct((seqs * spans, HEADS, HV, HK), BF16)],
        compiler_params=params(32),
        cost_estimate=cost(2e10, 16 * MIB),
        name="attend",
    )(segs.reshape(-1), q, k, v, logit, seg_c, seg_r)


def attend_back_kernel(
    spans, seg_ref, q_ref, k_ref, v_ref, logit_ref, dc_ref, dr_ref, states_ref, g_ref,
    gq_ref, gk_ref, gv_ref, gl_ref, grad_state,
):
    i = spans - 1 - pl.program_id(1)
    at = (pl.program_id(0) * spans + i) * CH
    last_doc, prev_doc = span_docs(seg_ref, at, i == 0)

    @pl.when(pl.program_id(1) == 0)
    def _():
        grad_state[...] = jnp.zeros_like(grad_state)

    mask, rise, fall, growth, to_end, enter, same, keep = span_parts(
        logit_ref[...], dc_ref[...], dr_ref[0], last_doc, prev_doc
    )
    query = q_ref[...].astype(F32)
    keys = k_ref[...].astype(F32)
    qs = (query * rise).astype(BF16)
    ks = (keys * fall).astype(BF16)
    qg = (query * growth * enter).astype(BF16)
    kw = (keys * to_end * same).astype(BF16)
    keep = keep * jnp.where(last_doc == prev_doc, 1.0, 0.0)
    last_row = lax.broadcasted_iota(jnp.int32, (CH, HK), 0) == CH - 1
    upper = lax.broadcasted_iota(jnp.int32, (CH, CH), 0) <= lax.broadcasted_iota(jnp.int32, (CH, CH), 1)
    upper = upper.astype(F32)
    for h in range(HEADS):
        a, b = h * HK, (h + 1) * HK
        va = v_ref[:, h * HV : (h + 1) * HV]
        ga = g_ref[:, h * HV : (h + 1) * HV]
        qh, kh = qs[:, a:b], ks[:, a:b]
        state = states_ref[0, h]
        grad = grad_state[h]
        grad_low = grad.astype(BF16)
        scores = (dot_nt(qh, kh) * mask).astype(BF16)
        grad_scores = (dot_nt(ga, va) * mask).astype(BF16)
        gv_ref[:, h * HV : (h + 1) * HV] = (dot_tn(scores, ga) + dot_nt(kw[:, a:b], grad_low)).astype(BF16)
        wk = dot(va, grad_low) * same * to_end[:, a:b]
        wq = dot(ga, state) * enter * growth[:, a:b]
        query_inner = dot(grad_scores, kh)
        key_inner = dot_tn(grad_scores, qh)
        gq_ref[:, a:b] = (query_inner * rise[:, a:b] + wq).astype(BF16)
        gk_ref[:, a:b] = (key_inner * fall[:, a:b] + wk).astype(BF16)
        ends = wk * keys[:, a:b]
        grad_cumul = qh.astype(F32) * query_inner - kh.astype(F32) * key_inner + query[:, a:b] * wq - ends
        kept = grad * keep[:, a:b]
        at_last = jnp.sum(ends, axis=0, keepdims=True) + jnp.sum(kept * state.astype(F32), axis=0, keepdims=True)
        grad_cumul = grad_cumul + jnp.where(last_row, at_last, 0.0)
        gl_ref[:, a:b] = dot(upper, grad_cumul, HIGH)
        grad_state[h] = kept + dot_tn(ga, qg[:, a:b])


def attend_back(q, k, v, logit, segs, seg_c, seg_r, states, grad):
    tokens = q.shape[0]
    seqs = segs.shape[0]
    spans = tokens // seqs // CH

    def part(width):
        return pl.BlockSpec((CH, width), lambda s, i, seg: (s * spans + spans - 1 - i, 0))

    return pl.pallas_call(
        functools.partial(attend_back_kernel, spans),
        grid_spec=pltpu.PrefetchScalarGridSpec(
            num_scalar_prefetch=1,
            grid=(seqs, spans),
            in_specs=[
                part(K),
                part(K),
                part(V),
                part(K),
                part(1),
                pl.BlockSpec((1, 1, CH), lambda s, i, seg: (s * spans + spans - 1 - i, 0, 0)),
                pl.BlockSpec((1, HEADS, HV, HK), lambda s, i, seg: (s * spans + spans - 1 - i, 0, 0, 0)),
                part(V),
            ],
            out_specs=[part(K), part(K), part(V), part(K)],
            scratch_shapes=[pltpu.VMEM((HEADS, HV, HK), F32)],
        ),
        out_shape=[
            struct((tokens, K), BF16),
            struct((tokens, K), BF16),
            struct((tokens, V), BF16),
            struct((tokens, K), F32),
        ],
        compiler_params=params(32),
        cost_estimate=cost(5e10, 20 * MIB),
        name="attend_back",
    )(segs.reshape(-1), q, k, v, logit, seg_c, seg_r, states, grad)


def mix_kernel(x_ref, n_ref, mixed_ref, w_ref, hg_ref, g2_ref, og_ref, gated_ref, middle_ref, n2_ref):
    normed = n_ref[...]
    outs = [None] * 4
    for c in range(HEADS):
        og = None
        for r in range(2):
            for core in range(2):
                at = r * 512 + core * 256
                part = dot(normed[:, at : at + 256], w_ref[core, r, c, :, :HV])
                og = part if og is None else og + part
        og_ref[:, c * HV : (c + 1) * HV] = og
        mixed = mixed_ref[:, c * HV : (c + 1) * HV]
        inverse = lax.rsqrt(jnp.mean(mixed * mixed, axis=-1, keepdims=True) + EPS)
        gated = (mixed * inverse * hg_ref[...] * (og * jax.nn.sigmoid(og))).astype(BF16)
        gated_ref[:, c * HV : (c + 1) * HV] = gated
        for e in range(4):
            part = dot(gated, w_ref[c % 2, c // 2, e, :, HV:])
            outs[e] = part if outs[e] is None else outs[e] + part
    middle = x_ref[...].astype(F32) + jnp.concatenate(outs, axis=1)
    middle_ref[...] = middle
    inverse = lax.rsqrt(jnp.mean(middle * middle, axis=-1, keepdims=True) + EPS)
    n2_ref[...] = (middle * inverse * g2_ref[...]).astype(BF16)


def mix(x, normed, mixed, weights, head_gain, gain_two):
    tokens = x.shape[0]
    return pl.pallas_call(
        mix_kernel,
        grid=(tokens // TILE,),
        in_specs=[
            rows(TILE, D),
            rows(TILE, D),
            rows(TILE, V),
            fixed((2, 2, 4, 256, 512)),
            fixed((1, HV)),
            fixed((1, D)),
        ],
        out_specs=[rows(TILE, V), rows(TILE, V), rows(TILE, D), rows(TILE, D)],
        out_shape=[
            struct((tokens, V), F32),
            struct((tokens, V), BF16),
            struct((tokens, D), F32),
            struct((tokens, D), BF16),
        ],
        compiler_params=params(48),
        cost_estimate=cost(2 * tokens * D * 2048, 24 * MIB),
        name="mix",
    )(x, normed, mixed, weights, head_gain, gain_two)


def feed_kernel(
    core_ref, n2_ref, dy_ref, middle_ref, gl_ref, dn_ref,
    out_ref, gn_ref, keep_gl, send_gl, keep_dn, send_dn, y_acc, hid, gate_g, lift_g,
):
    step = pl.program_id(0)
    core = core_ref[0]

    @pl.loop(0, n2_ref.shape[0] // TILE)
    def _(t):
        at = pl.ds(pl.multiple_of(t * TILE, TILE), TILE)
        gate = lift = back = None
        for r in range(2):
            n2 = n2_ref[at, r * 512 : (r + 1) * 512]
            a = dot_nt(n2, gl_ref[:, r, 0, :176].reshape(HC, 512))
            b = dot_nt(n2, gl_ref[:, r, 0, 176:].reshape(HC, 512))
            gate = a if r == 0 else gate + a
            lift = b if r == 0 else lift + b
        for c in range(4):
            a = dot_nt(dy_ref[at, c * 256 : (c + 1) * 256], dn_ref[:, 0, c].reshape(HC, 256))
            back = a if c == 0 else back + a
        sig = jax.nn.sigmoid(gate)
        swish = gate * sig
        hidden = (swish * lift).astype(BF16)
        grad_lift = (back * swish).astype(BF16)
        grad_gate = (back * lift * sig * (1.0 + gate * (1.0 - sig))).astype(BF16)
        hid[at, :] = hidden
        gate_g[at, :] = grad_gate
        lift_g[at, :] = grad_lift
        for c in range(4):
            part = dot(hidden, dn_ref[:, 0, c].reshape(HC, 256))
            lanes = slice(c * 256, (c + 1) * 256)

            @pl.when(step == 0)
            def _():
                y_acc[at, lanes] = part

            @pl.when(step > 0)
            def _():
                y_acc[at, lanes] += part

        for r in range(2):
            part = dot(grad_gate, gl_ref[:, r, 0, :176].reshape(HC, 512)) + dot(
                grad_lift, gl_ref[:, r, 0, 176:].reshape(HC, 512)
            )
            lanes = slice(r * 512, (r + 1) * 512)

            @pl.when(step == 0)
            def _():
                gn_ref[at, lanes] = part

            @pl.when(step > 0)
            def _():
                gn_ref[at, lanes] += part

        @pl.when(step == 3)
        def _():
            out_ref[at, :] = (middle_ref[at, :] + y_acc[at, :]).astype(BF16)

    first = core == 0
    for r in range(2):
        n2 = n2_ref[:, r * 512 : (r + 1) * 512]
        for m, source in enumerate((gate_g, lift_g)):
            both = dot_tn(source[...], n2).astype(BF16)
            low, high = both[: HC // 2], both[HC // 2 :]
            mine = jnp.where(first, low, high)
            other = jnp.where(first, high, low)
            for x in range(2):
                keep_gl[x, r, 0, m * 176 : (m + 1) * 176] = mine[x * 176 : (x + 1) * 176]
                send_gl[x, r, 0, m * 176 : (m + 1) * 176] = other[x * 176 : (x + 1) * 176]
    for c in range(4):
        both = dot_tn(hid[...], dy_ref[:, c * 256 : (c + 1) * 256]).astype(BF16)
        low, high = both[: HC // 2], both[HC // 2 :]
        mine = jnp.where(first, low, high)
        other = jnp.where(first, high, low)
        for x in range(2):
            keep_dn[x, 0, c, 0] = mine[x * 176 : (x + 1) * 176]
            send_dn[x, 0, c, 0] = other[x * 176 : (x + 1) * 176]


def feed(core, n2, dy, middle, weights):
    tokens = n2.shape[0]
    gl = pl.BlockSpec((2, 2, 1, 352, 512), lambda i, c: (0, 0, i, 0, 0))
    dn = pl.BlockSpec((2, 1, 4, 1, 176, 256), lambda i, c: (0, i // 2, 0, i % 2, 0, 0))
    once = pl.Buffered(1)
    return pl.pallas_call(
        feed_kernel,
        grid_spec=pltpu.PrefetchScalarGridSpec(
            num_scalar_prefetch=1,
            grid=(4,),
            in_specs=[
                pl.BlockSpec((tokens, D), lambda i, c: (0, 0), pipeline_mode=once),
                pl.BlockSpec((tokens, D), lambda i, c: (0, 0), pipeline_mode=once),
                pl.BlockSpec((tokens, D), lambda i, c: (0, 0), pipeline_mode=once),
                pl.BlockSpec((4, 2, 1, 352, 512), lambda i, c: (0, 0, i, 0, 0)),
                pl.BlockSpec((2, 1, 4, 352, 256), lambda i, c: (i % 2, i // 2, 0, 0, 2)),
            ],
            out_specs=[
                pl.BlockSpec((tokens, D), lambda i, c: (0, 0), pipeline_mode=once),
                pl.BlockSpec((tokens, D), lambda i, c: (0, 0), pipeline_mode=once),
                gl,
                gl,
                dn,
                dn,
            ],
            scratch_shapes=[
                pltpu.VMEM((tokens, D), F32),
                pltpu.VMEM((tokens, HC), BF16),
                pltpu.VMEM((tokens, HC), BF16),
                pltpu.VMEM((tokens, HC), BF16),
            ],
        ),
        out_shape=[
            struct((tokens, D), BF16),
            struct((tokens, D), F32),
            struct((2, 2, 4, 352, 512), BF16),
            struct((2, 2, 4, 352, 512), BF16),
            struct((2, 2, 4, 2, 176, 256), BF16),
            struct((2, 2, 4, 2, 176, 256), BF16),
        ],
        compiler_params=params(60),
        cost_estimate=cost(18 * tokens * D * FF, 60 * MIB),
        name="feed",
    )(core, n2, dy, middle, weights, weights)


def unmix_kernel(
    gn_ref, middle_ref, dy_ref, og_ref, mixed_ref, w_ref, hg_ref, g2_ref,
    gm_ref, gb_ref, gog_ref, gmix_ref, gg2_ref, ghg_ref,
):
    @pl.when(pl.program_id(0) == 0)
    def _():
        gg2_ref[...] = jnp.zeros_like(gg2_ref)
        ghg_ref[...] = jnp.zeros_like(ghg_ref)

    grad = gn_ref[...]
    middle = middle_ref[...]
    inverse = lax.rsqrt(jnp.mean(middle * middle, axis=-1, keepdims=True) + EPS)
    unit = middle * inverse
    gg2_ref[...] += jnp.sum(grad * unit, axis=0, keepdims=True)
    scaled = grad * g2_ref[...]
    grad_middle = dy_ref[...].astype(F32) + inverse * (scaled - unit * jnp.mean(scaled * unit, axis=-1, keepdims=True))
    gm_ref[...] = grad_middle
    branch = grad_middle.astype(BF16)
    gb_ref[...] = branch
    head_gain = hg_ref[...]
    for c in range(HEADS):
        lanes = slice(c * HV, (c + 1) * HV)
        back = None
        for e in range(4):
            part = dot_nt(branch[:, e * 256 : (e + 1) * 256], w_ref[c % 2, c // 2, e, :, HV:])
            back = part if back is None else back + part
        og = og_ref[:, lanes]
        sig = jax.nn.sigmoid(og)
        mixed = mixed_ref[:, lanes]
        inv = lax.rsqrt(jnp.mean(mixed * mixed, axis=-1, keepdims=True) + EPS)
        unit = mixed * inv
        gog_ref[:, lanes] = (back * (unit * head_gain) * sig * (1.0 + og * (1.0 - sig))).astype(BF16)
        incoming = back * (og * sig)
        ghg_ref[...] += jnp.sum(incoming * unit, axis=0, keepdims=True)
        scaled = incoming * head_gain
        gmix_ref[:, lanes] = (inv * (scaled - unit * jnp.mean(scaled * unit, axis=-1, keepdims=True))).astype(BF16)


def unmix(grad, middle, dy, og, mixed, weights, head_gain, gain_two):
    tokens = grad.shape[0]
    return pl.pallas_call(
        unmix_kernel,
        grid=(tokens // TILE,),
        in_specs=[
            rows(TILE, D),
            rows(TILE, D),
            rows(TILE, D),
            rows(TILE, V),
            rows(TILE, V),
            fixed((2, 2, 4, 256, 512)),
            fixed((1, HV)),
            fixed((1, D)),
        ],
        out_specs=[rows(TILE, D), rows(TILE, D), rows(TILE, V), rows(TILE, V), fixed((1, D)), fixed((1, HV))],
        out_shape=[
            struct((tokens, D), F32),
            struct((tokens, D), BF16),
            struct((tokens, V), BF16),
            struct((tokens, V), BF16),
            struct((1, D), F32),
            struct((1, HV), F32),
        ],
        compiler_params=params(56),
        cost_estimate=cost(2 * tokens * D * D, 30 * MIB),
        name="unmix",
    )(grad, middle, dy, og, mixed, weights, head_gain, gain_two)


def weight_grad_kernel(plan, core_ref, *refs):
    count = 2 * len(plan)
    keep_ref, send_ref = refs[-2:]
    lefts, rights = refs[:count], refs[count:-2]
    for j, (lefts_at, groups) in enumerate(plan):
        for start, index, width in groups:
            right = rights[index][...]
            for ref, left in ((keep_ref, lefts[2 * lefts_at]), (send_ref, lefts[2 * lefts_at + 1])):
                part = dot_tn(left[...], right).astype(BF16)
                for x in range(2):
                    ref[x, 0, 0, :, start : start + width] = part[x * 128 : (x + 1) * 128]


def weight_grads(core, lefts, rights, plan):
    tokens = lefts[0].shape[0]
    specs = []
    for left in lefts:
        specs.append(pl.BlockSpec((tokens, 256), lambda r, c, core: (0, r * 2 + core[0])))
        specs.append(pl.BlockSpec((tokens, 256), lambda r, c, core: (0, r * 2 + 1 - core[0])))
    for right in rights:
        specs.append(pl.BlockSpec((tokens, right.shape[1] // 4), lambda r, c, core: (0, c)))
    out = pl.BlockSpec((2, 1, 1, 128, 512), lambda r, c, core: (0, r, c, 0, 0))
    operands = [left for left in lefts for _ in range(2)] + list(rights)
    return pl.pallas_call(
        functools.partial(weight_grad_kernel, plan),
        grid_spec=pltpu.PrefetchScalarGridSpec(
            num_scalar_prefetch=1, grid=(2, 4), in_specs=specs, out_specs=[out, out]
        ),
        out_shape=[struct((2, 2, 4, 128, 512), BF16)] * 2,
        compiler_params=params(40),
        cost_estimate=cost(2 * tokens * D * 2048, 12 * MIB),
        name="weight_grads",
    )(core, *operands)


def unproject_kernel(
    x_ref, n_ref, gq_ref, gk_ref, gv_ref, glog_ref, logit_ref, low_ref, gog_ref, gm_ref,
    w_ref, wo_ref, ddt_ref, du_ref, g1_ref,
    gx_ref, gddt_ref, gdu_ref, gbias_ref, gg1_ref,
):
    @pl.when(pl.program_id(0) == 0)
    def _():
        gddt_ref[...] = jnp.zeros_like(gddt_ref)
        gdu_ref[...] = jnp.zeros_like(gdu_ref)
        gbias_ref[...] = jnp.zeros_like(gbias_ref)
        gg1_ref[...] = jnp.zeros_like(gg1_ref)

    normed = n_ref[...]
    grad_logit = glog_ref[...] * (1.0 / 16.0) * jax.nn.sigmoid(-logit_ref[...])
    gbias_ref[...] += jnp.sum(grad_logit, axis=0, keepdims=True)
    gdu_ref[...] += dot_tn(low_ref[...], grad_logit, HIGH)
    grad_low = dot_nt(grad_logit, du_ref[...], HIGH).astype(BF16)
    gddt_ref[...] += dot_tn(grad_low, normed)
    parts = []
    for r in range(2):
        small = dot(grad_low, ddt_ref[r])
        for core in range(2):
            total = small[:, core * 256 : (core + 1) * 256]
            for c in range(HEADS):
                w = w_ref[core, r, c]
                total = total + dot_nt(gq_ref[:, c * HK : (c + 1) * HK], w[:, :HK])
                total = total + dot_nt(gk_ref[:, c * HK : (c + 1) * HK], w[:, HK : 2 * HK])
                total = total + dot_nt(gv_ref[:, c * HV : (c + 1) * HV], w[:, 2 * HK :])
                total = total + dot_nt(gog_ref[:, c * HV : (c + 1) * HV], wo_ref[core, r, c])
            parts.append(total)
    grad = jnp.concatenate(parts, axis=1)
    x = x_ref[...].astype(F32)
    inverse = lax.rsqrt(jnp.mean(x * x, axis=-1, keepdims=True) + EPS)
    unit = x * inverse
    gg1_ref[...] += jnp.sum(grad * unit, axis=0, keepdims=True)
    scaled = grad * g1_ref[...]
    gx_ref[...] = gm_ref[...] + inverse * (scaled - unit * jnp.mean(scaled * unit, axis=-1, keepdims=True))


def unproject(x, normed, gq, gk, gv, glog, logit, low, gog, gm, weights, out_weights, ddt, du, gain):
    tokens = x.shape[0]
    return pl.pallas_call(
        unproject_kernel,
        grid=(tokens // TILE,),
        in_specs=[
            rows(TILE, D),
            rows(TILE, D),
            rows(TILE, K),
            rows(TILE, K),
            rows(TILE, V),
            rows(TILE, K),
            rows(TILE, K),
            rows(TILE, LOW),
            rows(TILE, V),
            rows(TILE, D),
            fixed((2, 2, 4, 256, 512)),
            fixed((2, 2, 4, 256, HV)),
            fixed((2, LOW, 512)),
            fixed((LOW, K)),
            fixed((1, D)),
        ],
        out_specs=[rows(TILE, D), fixed((LOW, D)), fixed((LOW, K)), fixed((1, K)), fixed((1, D))],
        out_shape=[
            struct((tokens, D), F32),
            struct((LOW, D), F32),
            struct((LOW, K), F32),
            struct((1, K), F32),
            struct((1, D), F32),
        ],
        compiler_params=params(56),
        cost_estimate=cost(2 * tokens * D * 3072, 30 * MIB),
        name="unproject",
    )(x, normed, gq, gk, gv, glog, logit, low, gog, gm, weights, out_weights, ddt, du, gain)


def ring_gather(part, axis, count):
    me = lax.axis_index(axis)
    if count == 2:
        other = lax.ppermute(part, axis, [(0, 1), (1, 0)])
        first = me == 0
        return jnp.stack([jnp.where(first, part, other), jnp.where(first, other, part)])
    whole = jnp.zeros((count,) + part.shape, part.dtype)
    whole = lax.dynamic_update_index_in_dim(whole, part, me, 0)
    moving = part
    for step in range(1, count):
        moving = lax.ppermute(moving, axis, [(i, (i + 1) % count) for i in range(count)])
        whole = lax.dynamic_update_index_in_dim(whole, moving, lax.rem(me + count - step, count), 0)
    return whole


def added(parts):
    total = parts[0].astype(F32)
    for part in parts[1:]:
        total = total + part.astype(F32)
    return total.astype(BF16)


def scatter_add(arrays, axis, count):
    me = lax.axis_index(axis)

    def piece(place):
        return added([lax.dynamic_index_in_dim(array, place, 0, keepdims=False) for array in arrays])

    received = []
    for shift in range(1, count):
        going = piece(lax.rem(me + shift, count))
        received.append(lax.ppermute(going, axis, [(i, (i + shift) % count) for i in range(count)]))
    return [piece(me)] + received


def reduce_pack(keep, send, rows_count, cols_count):
    arrays = [keep, lax.ppermute(send, "core", [(0, 1), (1, 0)])]
    arrays = scatter_add(arrays, "x", 2)
    arrays = scatter_add(arrays, "row", rows_count)
    arrays = scatter_add(arrays, "col", cols_count)
    total = added(arrays)
    return ring_gather(ring_gather(total, "x", 2), "core", 2)


def small_block(ddt, du, bias, g1, hg, g2):
    first = jnp.concatenate([ddt, jnp.pad(du, ((0, 0), (0, 512 - du.shape[1])))], axis=0)
    line = jnp.concatenate([jnp.pad(bias, (0, 64)), g1, jnp.pad(hg, (0, 96)), g2])
    return jnp.concatenate([first, line.reshape(1, 512), jnp.zeros((3, 512), first.dtype)], axis=0)


def per_device(
    layer_input,
    segment_ids,
    norm1_gain,
    query_weight,
    key_weight,
    value_weight,
    outgate_weight,
    decay_down,
    decay_up,
    decay_bias,
    head_gain,
    out_weight,
    norm2_gain,
    swiglu_gate,
    swiglu_up,
    swiglu_down,
    cotangent,
):
    row_count = lax.axis_size("row")
    col_count = lax.axis_size("col")
    fast = row_count == 2 and col_count == 4 and lax.axis_size("x") == 2
    core = lax.axis_index("core")
    quarter = lax.axis_index("x") * 2 + core
    owned = (query_weight, key_weight, value_weight, outgate_weight, out_weight)

    if fast:
        feed_rows = jnp.concatenate(
            [
                jnp.concatenate(
                    [
                        lax.dynamic_slice_in_dim(swiglu_gate.T, quarter * 176, 176, 0),
                        lax.dynamic_slice_in_dim(swiglu_up.T, quarter * 176, 176, 0),
                    ],
                    axis=0,
                ),
                lax.dynamic_slice_in_dim(swiglu_down, quarter * 352, 352, 0),
            ],
            axis=1,
        )
        feed_full = lax.all_gather(feed_rows, AXES, axis=0, tiled=True).reshape(4, 2, 4, 352, 768)

        def gather(part):
            part = ring_gather(ring_gather(part, "col", col_count), "row", row_count)
            return ring_gather(part, "core", 2)

        qkv = jnp.concatenate([query_weight, key_weight, value_weight], axis=1)
        qkv = lax.dynamic_slice_in_dim(qkv, core * 256, 256, 0)
        small = small_block(decay_down.T, decay_up, decay_bias, norm1_gain, head_gain, norm2_gain)
        qkv_full = gather(jnp.concatenate([qkv, small], axis=0))
        ogout = jnp.concatenate([outgate_weight, out_weight], axis=1)
        ogout_full = gather(lax.dynamic_slice_in_dim(ogout, core * 256, 256, 0))
        small = qkv_full[0, :, :, 256:]
        ddt = small[:, :, :4].reshape(2, LOW, 512)
        du = small[:, :, 4:12, :HK].transpose(0, 2, 1, 3).reshape(LOW, K)
        bias = small[:, :, 12, :64].reshape(1, K)
        g1 = small[:, :, 12, 128:256].reshape(1, D)
        hg = small[:, :, 12, 256:288].reshape(1, HV)
        g2 = small[:, :, 12, 384:].reshape(1, D)
    else:

        def whole(shard):
            if shard.ndim == 1:
                return lax.all_gather(shard, ("row", "col"), axis=0, tiled=True)
            wide = lax.all_gather(shard, "col", axis=1, tiled=True)
            return lax.all_gather(wide, "row", axis=0, tiled=True)

        def blocks(full, width):
            return full.reshape(2, 2, 256, 4, width).transpose(1, 0, 3, 2, 4)

        qkv_full = jnp.concatenate(
            [blocks(whole(query_weight), 128), blocks(whole(key_weight), 128), blocks(whole(value_weight), 256)],
            axis=-1,
        )
        ogout_full = jnp.concatenate([blocks(whole(outgate_weight), 256), blocks(whole(out_weight), 256)], axis=-1)
        gate_t, lift_t, down = whole(swiglu_gate).T, whole(swiglu_up).T, whole(swiglu_down)
        feed_gate = gate_t.reshape(4, 4, 176, 2, 512).transpose(1, 3, 0, 2, 4)
        feed_lift = lift_t.reshape(4, 4, 176, 2, 512).transpose(1, 3, 0, 2, 4)
        feed_down = down.reshape(2, 4, 352, 4, 256).transpose(1, 0, 3, 2, 4)
        feed_full = jnp.concatenate([jnp.concatenate([feed_gate, feed_lift], axis=3), feed_down], axis=-1)
        ddt = whole(decay_down).T.reshape(LOW, 2, 512).transpose(1, 0, 2)
        du = whole(decay_up)
        bias = whole(decay_bias).reshape(1, K)
        g1 = whole(norm1_gain).reshape(1, D)
        hg = whole(head_gain).reshape(1, HV)
        g2 = whole(norm2_gain).reshape(1, D)
    du, bias, g1, hg, g2 = (part.astype(F32) for part in (du, bias, g1, hg, g2))

    tokens = layer_input.shape[0]
    seg_c = segment_ids.reshape(tokens, 1)
    seg_r = segment_ids.reshape(tokens // CH, 1, CH)
    core_at = (core if fast else jnp.zeros_like(core)).astype(jnp.int32).reshape(1)

    normed, q, k, v, low, logit = project(layer_input, g1, qkv_full, ddt, du, bias)
    mixed, states = attend(q, k, v, logit, segment_ids, seg_c, seg_r)
    og, gated, middle, normed_two = mix(layer_input, normed, mixed, ogout_full, hg, g2)
    layer_output, grad_normed_two, keep_gl, send_gl, keep_dn, send_dn = feed(
        core_at, normed_two, cotangent, middle, feed_full
    )
    grad_middle, branch, grad_og, grad_mixed, grad_g2, grad_hg = unmix(
        grad_normed_two, middle, cotangent, og, mixed, ogout_full, hg, g2
    )
    keep_oo, send_oo = weight_grads(
        core_at, [normed, gated], [grad_og, branch], ((0, ((0, 0, 256),)), (1, ((256, 1, 256),)))
    )
    gq, gk, gv, glog = attend_back(q, k, v, logit, segment_ids, seg_c, seg_r, states, grad_mixed)
    keep_qkv, send_qkv = weight_grads(
        core_at, [normed], [gq, gk, gv], ((0, ((0, 0, 128), (128, 1, 128), (256, 2, 256))),)
    )
    input_grad, grad_ddt, grad_du, grad_bias, grad_g1 = unproject(
        layer_input, normed, gq, gk, gv, glog, logit, low, grad_og, grad_middle, qkv_full, ogout_full, ddt, du, g1
    )

    tiny = jnp.concatenate(
        [
            grad_ddt,
            jnp.pad(grad_du, ((0, 0), (0, D - K))),
            jnp.concatenate([grad_bias, grad_hg, jnp.zeros((1, D - K - HV), F32)], axis=1),
            grad_g1,
            grad_g2,
            jnp.zeros((5, D), F32),
        ],
        axis=0,
    )
    tiny = lax.psum(tiny, AXES)
    r, c = lax.axis_index("row"), lax.axis_index("col")

    def own(line, size):
        return lax.dynamic_slice_in_dim(line, (r * col_count + c) * size, size, 0)

    def own_block(full, shape):
        return lax.dynamic_slice(full, (r * shape[0], c * shape[1]), shape)

    out_bias = own(tiny[32, :K], decay_bias.shape[0])
    out_hg = own(tiny[32, K : K + HV], head_gain.shape[0])
    out_g1 = own(tiny[33], norm1_gain.shape[0])
    out_g2 = own(tiny[34], norm2_gain.shape[0])
    out_du = own_block(tiny[16:32, :K], decay_up.shape)
    down_rows = decay_down.shape
    out_dd = lax.dynamic_slice(tiny, (c * down_rows[1], r * down_rows[0]), down_rows[::-1]).T

    if fast:
        gl = reduce_pack(keep_gl, send_gl, row_count, col_count)
        dn = reduce_pack(keep_dn, send_dn, row_count, col_count)
        oo = reduce_pack(keep_oo, send_oo, row_count, col_count)
        qkv = reduce_pack(keep_qkv, send_qkv, row_count, col_count)
        gl = gl.reshape(2, 2, 2, 176, 512).transpose(2, 0, 1, 3, 4).reshape(2, HC, 512)
        out_gate, out_lift = gl[0].T, gl[1].T
        out_down = dn.transpose(2, 0, 1, 3, 4).reshape(1408, 256)
        oo = oo.reshape(512, 512)
        qkv = qkv.reshape(512, 512)
        shards = [qkv[:, :128], qkv[:, 128:256], qkv[:, 256:], oo[:, :256], oo[:, 256:], out_gate, out_lift, out_down]
    else:

        def joined(keep, send):
            return jnp.stack([keep, send])

        def matrix(pack):
            return pack.transpose(2, 0, 1, 4, 3, 5).reshape(D, -1)

        oo = joined(keep_oo, send_oo)
        qkv = joined(keep_qkv, send_qkv)
        gl = joined(keep_gl, send_gl).reshape(2, 2, 2, 4, 2, 176, 512).transpose(4, 3, 0, 1, 5, 2, 6)
        gl = gl.reshape(2, FF, D)
        dn = joined(keep_dn, send_dn).transpose(2, 4, 0, 1, 5, 3, 6).reshape(FF, D)
        fulls = [
            matrix(qkv[..., :128]),
            matrix(qkv[..., 128:256]),
            matrix(qkv[..., 256:]),
            matrix(oo[..., :256]),
            matrix(oo[..., 256:]),
            gl[0].T,
            gl[1].T,
            dn,
        ]
        shards = []
        for full in fulls:
            part = lax.psum(full, ("x", "core"))
            part = lax.psum_scatter(part, "row", scatter_dimension=0, tiled=True)
            shards.append(lax.psum_scatter(part, "col", scatter_dimension=1, tiled=True))
    out_q, out_k, out_v, out_og, out_out, out_gate, out_lift, out_down = (part.astype(F32) for part in shards)
    return (
        layer_output,
        input_grad,
        out_g1,
        out_q,
        out_k,
        out_v,
        out_og,
        out_dd,
        out_du,
        out_bias,
        out_hg,
        out_out,
        out_g2,
        out_gate,
        out_lift,
        out_down,
    )


def solution(mesh):
    shape = dict(mesh.shape)
    finer = Mesh(mesh.devices.reshape(shape["dp"] // 2, 2, shape["row"], shape["col"]), AXES)
    tokens = P(AXES, None)
    vector = P(("row", "col"))
    matrix = P("row", "col")
    in_specs = (
        tokens, tokens, vector, matrix, matrix, matrix, matrix, matrix, matrix, vector, vector,
        matrix, vector, matrix, matrix, matrix, tokens,
    )
    out_specs = (
        tokens, tokens, vector, matrix, matrix, matrix, matrix, matrix, matrix, vector, vector,
        matrix, vector, matrix, matrix, matrix,
    )
    return jax.shard_map(per_device, mesh=finer, in_specs=in_specs, out_specs=out_specs, check_vma=False)
```

time: 3780 us -> 701 us (0.19)
  blocking collectives: 2080 us -> 0 us
  local copies, waits for them, and re-layouts: 529 us -> 34.6 us
  other arithmetic: 480 us -> 54.2 us
  matrix products: 408 us -> 0 us
  Pallas kernels: 0 us -> 209 us
  waiting for transfers between devices: 216 us -> 319 us
  starting transfers between devices: 0.37 us -> 64.5 us
    unnamed x2 -> x0, blocking collectives: 1980 us -> none
    dot_general x238 -> x0, matrix products: 408 us -> none  [the longest x9 70.6 us: back_matmul(): jnp.einsum('tq,pq->tp', left, right, preferred_element_type=jnp.float32)]
    pallas_call x0 -> x9, Pallas kernels: none -> 209 us  [the longest x1 91.7 us: feed(): pl.pallas_call(feed_kernel, grid_spec=pltpu.PrefetchScalarGridSpec(num_sc...]
    ppermute x0 -> x42, waiting for transfers between devices: none -> 197 us  [the longest x20 97.2 us: scatter_add(): lax.ppermute(going, axis, [(i, (i + shift) % count) for i in range(count)])]
    all_gather x8 -> x1, waiting for transfers between devices: 179 us -> 0.01 us  [per_device(): lax.all_gather(feed_rows, AXES, axis=0, tiled=True)]
    all_gather x10 -> x0, other arithmetic: 167 us -> none  [the longest x1 36.1 us: per_device(): lax.all_gather(swiglu_down.reshape(1, -1), ('row', 'col'), axis=0, tiled=...]
    unnamed x231 -> x111, local copies, waits for them, and re-layouts: 174 us -> 18.7 us
    reshape x25 -> x4, local copies, waits for them, and re-layouts: 117 us -> 0.32 us  [the longest x1 0.22 us: per_device(): seg_c = segment_ids.reshape(tokens, 1)]
  transfers between devices with their start and end apart: 9 -> 44, of which waited for: 5 -> 20; matrix products, arithmetic and copies ran while one was open for 15% -> 9% of each run, Pallas kernels for 0% -> 17%
where the time goes in v1:
time: 701 us; the launch traced here: 697 us
  waiting for transfers between devices  319 us (46%)
  Pallas kernels  209 us (30%)
  starting transfers between devices  64.5 us (9%)
  other arithmetic  54.2 us (8%)
  local copies, waits for them, and re-layouts  34.6 us (5%)
  between operations  15.4 us (2%)
    psum x1, waiting for transfers between devices, per_device(): tiny = lax.psum(tiny, AXES)  121 us
    ppermute x20, waiting for transfers between devices, scatter_add(): lax.ppermute(going, axis, [(i, (i + shift) % count) for i in range(count)])  97.2 us
    pallas_call x1, Pallas kernels, feed(): pl.pallas_call(feed_kernel, grid_spec=pltpu.PrefetchScalarGridSpec(num_sc...  91.7 us
    ppermute x12, waiting for transfers between devices, ring_gather(): other = lax.ppermute(part, axis, [(0, 1), (1, 0)])  58.4 us
    ppermute x6, waiting for transfers between devices, ring_gather(): lax.ppermute(moving, axis, [(i, (i + 1) % count) for i in range(count)])  41.6 us
    ppermute x20, starting transfers between devices, scatter_add(): lax.ppermute(going, axis, [(i, (i + shift) % count) for i in range(count)])  29.7 us
    convert_element_type x16, other arithmetic, added(): return total.astype(BF16)  25.7 us
    pallas_call x1, Pallas kernels, attend_back(): pl.pallas_call(functools.partial(attend_back_kernel, spans), grid_spec=pl...  24.5 us
  transfers between devices with their start and end apart: 44, of which 20 were waited for; matrix products, arithmetic and copies ran while one was open for 9% of the time, Pallas kernels for 17%

profile of v1, /device:TPU:9, one launch (start us, length us, event | category | flops | bytes accessed | tf_op | source)
XLA Modules:
  0.0 696.6 jit_solution(2309016833217859895)
XLA Ops:
  19.3 5.3 collective-permute-done
  26.2 10.2 %collective-permute-done.6 = bf16[256,512]{1,0:T(8,128)(2,1)S(1)} collective-permute-done((bf16[256,512]{1,0:T(8,128)(2,1)S(1)}, bf16[256,512]{1,0:T(8,128)(2,1)S(1)}, u32[]{:S(2)}, u32[]{:S(2)}) %collective-permute-start.6) | collective-permute-done | bytes 262176 | tf_op jit(solution)/shard_map/ppermute | solution.py:653
  39.8 7.3 %collective-permute-done.1 = bf16[272,512]{1,0:T(8,128)(2,1)S(1)} collective-permute-done((bf16[272,512]{1,0:T(8,128)(2,1)S(1)}, bf16[272,512]{1,0:T(8,128)(2,1)S(1)}, u32[]{:S(2)}, u32[]{:S(2)}) %collective-permute-start.1) | collective-permute-done | bytes 278560 | tf_op jit(solution)/shard_map/ppermute | solution.py:653
  54.0 10.4 %collective-permute-done.2 = bf16[272,512]{1,0:T(8,128)(2,1)S(1)} collective-permute-done((bf16[272,512]{1,0:T(8,128)(2,1)S(1)}, bf16[272,512]{1,0:T(8,128)(2,1)S(1)}, u32[]{:S(2)}, u32[]{:S(2)}) %collective-permute-start.2) | collective-permute-done | bytes 278560 | tf_op jit(solution)/shard_map/ppermute | solution.py:653
  65.8 18.6 %collective-permute-done.8 = bf16[4,256,512]{2,1,0:T(8,128)(2,1)} collective-permute-done((bf16[4,256,512]{2,1,0:T(8,128)(2,1)S(1)}, bf16[4,256,512]{2,1,0:T(8,128)(2,1)}, u32[]{:S(2)}, u32[]{:S(2)}) %collective-permute-start.8) | collective-permute-done | bytes 1048608 | tf_op jit(solution)/shard_map/ppermute | solution.py:646
  90.4 33.9 %collective-permute-done.3 = bf16[4,272,512]{2,1,0:T(8,128)(2,1)} collective-permute-done((bf16[4,272,512]{2,1,0:T(8,128)(2,1)S(1)}, bf16[4,272,512]{2,1,0:T(8,128)(2,1)}, u32[]{:S(2)}, u32[]{:S(2)}) %collective-permute-start.3) | collective-permute-done | bytes 1114144 | tf_op jit(solution)/shard_map/ppermute | solution.py:646
  148.2 10.4 %project.1 = (bf16[1024,1024]{1,0:T(8,128)(2,1)S(1)}, bf16[1024,512]{1,0:T(8,128)(2,1)S(1)}, bf16[1024,512]{1,0:T(8,128)(2,1)S(1)}, bf16[1024,1024]{1,0:T(8,128)...) custom-call(bf16[1024,1024]{1,0:T(8,128)(2,1)S(1)} %copy-done.3, f32[1,1024]{1,0:T(1,128)S(1)} %convert.41.gain_ref.g1_ref, ...), custom_call_target="tpu_custom_call" | custom-call | flops 4294967296 | bytes 14680064 | tf_op jit(solution)/shard_map/project/pallas_call | solution.py:89
  160.8 14.5 %attend.1 = (f32[1024,1024]{1,0:T(8,128)S(1)}, bf16[16,4,256,128]{3,2,1,0:T(8,128)(2,1)S(1)}) custom-call(s32[1024]{0:T(1024)S(1)} %bitcast.242, bf16[1024,512]{1,0:T(8,128)(2,1)S(1)} %get-tuple-element.54.q_ref, bf16[1024,512]{1,0:T(8,128)(2,1)S(1)} %get-tuple-element.55.k_ref, bf16[1024,1024]{1,0:T(8,128)(2,1)S(1)} %get-tuple-element.56.v_ref, ...), custom_call_target="tpu_custom_call" | custom-call | flops 20000000000 | bytes 16777216 | tf_op jit(solution)/shard_map/attend/pallas_call | solution.py:175
  179.4 12.6 %mix.1 = (f32[1024,1024]{1,0:T(8,128)}, bf16[1024,1024]{1,0:T(8,128)(2,1)S(1)}, f32[1024,1024]{1,0:T(8,128)}, bf16[1024,1024]{1,0:T(8,128)(2,1)S(1)}) custom-call(bf16[1024,1024]{1,0:T(8,128)(2,1)} %x_ref.5, bf16[1024,1024]{1,0:T(8,128)(2,1)} %copy-done.4, f32[1024,1024]{1,0:T(8,128)} %copy-done.2, ...), custom_call_target="tpu_custom_call" | custom-call | flops 4294967296 | bytes 25165824 | tf_op jit(solution)/shard_map/mix/pallas_call | solution.py:316
  194.7 91.7 %feed.1 = (bf16[1024,1024]{1,0:T(8,128)(2,1)}, f32[1024,1024]{1,0:T(8,128)}, bf16[2,2,4,352,512]{4,3,2,1,0:T(8,128)(2,1)}, bf16[2,2,4,352,512]{4,3,2,1,0:T(8,128...) custom-call(s32[1]{0:T(128)} %bitcast.core_ref, ...), custom_call_target="tpu_custom_call" | custom-call | flops 53150220288 | bytes 62914560 | tf_op jit(solution)/shard_map/feed/pallas_call | solution.py:424
  286.4 14.6 %unmix.1 = (f32[1024,1024]{1,0:T(8,128)}, bf16[1024,1024]{1,0:T(8,128)(2,1)}, bf16[1024,1024]{1,0:T(8,128)(2,1)}, bf16[1024,1024]{1,0:T(8,128)(2,1)}, f32[1,1024]{1,0:T(1,128)}, /*index=5*/f32[1,256]{1,0:T(1,128)}) custom-call(f32[1024,1024]{1,0:T(8,128)} %get-tuple-element.63.gn_ref, f32[1024,1024]{1,0:T(8,128)} %get-tuple-element.60.middle_ref, ...), custom_call_target="tpu_custom_call" | custom-call | flops 2147483648 | bytes 31457280 | tf_op jit(solution)/shard_map/unmix/pallas_call | solution.py:505
  304.3 9.0 %weight_grads.3 = (bf16[2,2,4,128,512]{4,3,2,1,0:T(8,128)(2,1)S(1)}, bf16[2,2,4,128,512]{4,3,2,1,0:T(8,128)(2,1)}) custom-call(s32[1]{0:T(128)} %bitcast.core_ref, bf16[1024,1024]{1,0:T(8,128)(2,1)S(1)} %copy-done.5, bf16[1024,1024]{1,0:T(8,128)(2,1)S(1)} %copy-done.5, bf16[1024,1024]{1,0:T(8,128)(2,1)S(1)} %copy-done.25, bf16[1024,1024]{1,0:T(8,128)(2,1)S(1)} %copy-done.25, ...), custom_call_target="tpu_custom_call" | custom-call | flops 4294967296 | bytes 12582912 | tf_op jit(solution)/shard_map/weight_grads/pallas_call | solution.py:556
  316.0 24.5 %attend_back.1 = (bf16[1024,512]{1,0:T(8,128)(2,1)S(1)}, bf16[1024,512]{1,0:T(8,128)(2,1)S(1)}, bf16[1024,1024]{1,0:T(8,128)(2,1)S(1)}, f32[1024,512]{1,0:T(8,128)S(1)}) custom-call(s32[1024]{0:T(1024)S(1)} %bitcast.243, bf16[1024,512]{1,0:T(8,128)(2,1)S(1)} %copy-done.30, bf16[1024,512]{1,0:T(8,128)(2,1)S(1)} %copy-done.32, ...), custom_call_target="tpu_custom_call" | custom-call | flops 49999998976 | bytes 20971520 | tf_op jit(solution)/shard_map/attend_back/pallas_call | solution.py:260
  341.8 11.0 %weight_grads.2 = (bf16[2,2,4,128,512]{4,3,2,1,0:T(8,128)(2,1)S(1)}, bf16[2,2,4,128,512]{4,3,2,1,0:T(8,128)(2,1)}) custom-call(s32[1]{0:T(128)} %bitcast.core_ref, bf16[1024,1024]{1,0:T(8,128)(2,1)S(1)} %copy-done.5, bf16[1024,1024]{1,0:T(8,128)(2,1)S(1)} %copy-done.5, bf16[1024,512]{1,0:T(8,128)(2,1)S(1)} %get-tuple-element.66.gq_ref.refs_2_, ...), custom_call_target="tpu_custom_call" | custom-call | flops 4294967296 | bytes 12582912 | tf_op jit(solution)/shard_map/weight_grads/pallas_call | solution.py:556
  363.0 8.8 %add_convert_fusion.1 = (bf16[1,2,4,352,512]{4,3,2,1,0:T(8,128)(2,1)}, bf16[2,4,352,512]{3,2,1,0:T(8,128)(2,1)}) fusion(bf16[2,2,4,352,512]{4,3,2,1,0:T(8,128)(2,1)} %collective-permute-done.26, s32[]{:T(128)S(6)} %select_n.290, bf16[2,2,4,352,512]{4,3,2,1,0:T(8,128)(2,1)} %get-tuple-element.86, s32[]{:T(128)S(6)} %select_n.292), kind=kLoop, calls=%fused_computation.1 | loop fusion | flops 11534336 | bytes 17301512 | tf_op jit(solution)/shard_map/convert_element_type | solution.py:662
  373.0 21.0 %unproject.1 = (f32[1024,1024]{1,0:T(8,128)}, f32[16,1024]{1,0:T(8,128)}, f32[16,512]{1,0:T(8,128)}, f32[1,512]{1,0:T(1,128)}, f32[1,1024]{1,0:T(1,128)}) custom-call(bf16[1024,1024]{1,0:T(8,128)(2,1)} %x_ref.5, bf16[1024,1024]{1,0:T(8,128)(2,1)} %copy-done.4, bf16[1024,512]{1,0:T(8,128)(2,1)} %copy-done.13, bf16[1024,512]{1,0:T(8,128)(2,1)} %copy-done.14, ...), custom_call_target="tpu_custom_call" | custom-call | flops 6442450944 | bytes 31457280 | tf_op jit(solution)/shard_map/unproject/pallas_call | solution.py:609
  399.0 121.4 %all-reduce.6.cloned.1.call-done = f32[40,1024]{1,0:T(8,128)} async-done(((f32[40,1024]{1,0:T(8,128)}), f32[40,1024]{1,0:T(8,128)}) %all-reduce.6.cloned.1.call-update) | async-done | bytes 163856 | tf_op jit(solution)/shard_map/psum | solution.py:817
  543.9 5.4 collective-permute-start.15
  557.1 6.6 collective-permute-done.22
  577.8 45.0 %collective-permute-done.36 = bf16[4,2,176,256]{3,2,1,0:T(8,128)(2,1)S(1)} collective-permute-done((bf16[4,2,176,256]{3,2,1,0:T(8,128)(2,1)S(1)}, bf16[4,2,176,256]{3,2,1,0:T(8,128)(2,1)S(1)}, u32[]{:S(2)}, u32[]{:S(2)}) %collective-permute-start.36) | collective-permute-done | bytes 720928 | tf_op jit(solution)/shard_map/ppermute | solution.py:674
  632.5 7.8 %collective-permute-done.38 = bf16[2,176,256]{2,1,0:T(8,128)(2,1)S(1)} collective-permute-done((bf16[2,176,256]{2,1,0:T(8,128)(2,1)S(1)}, bf16[2,176,256]{2,1,0:T(8,128)(2,1)S(1)}, u32[]{:S(2)}, u32[]{:S(2)}) %collective-permute-start.38) | collective-permute-done | bytes 180256 | tf_op jit(solution)/shard_map/ppermute | solution.py:674
  640.3 16.7 %collective-permute-done.39 = bf16[2,176,256]{2,1,0:T(8,128)(2,1)S(1)} collective-permute-done((bf16[2,176,256]{2,1,0:T(8,128)(2,1)S(1)}, bf16[2,176,256]{2,1,0:T(8,128)(2,1)S(1)}, u32[]{:S(2)}, u32[]{:S(2)}) %collective-permute-start.39) | collective-permute-done | bytes 180256 | tf_op jit(solution)/shard_map/ppermute | solution.py:674
  663.4 7.7 %collective-permute-done.30 = bf16[352,512]{1,0:T(8,128)(2,1)S(1)} collective-permute-done((bf16[352,512]{1,0:T(8,128)(2,1)S(1)}, bf16[352,512]{1,0:T(8,128)(2,1)S(1)}, u32[]{:S(2)}, u32[]{:S(2)}) %collective-permute-start.30) | collective-permute-done | bytes 360480 | tf_op jit(solution)/shard_map/ppermute | solution.py:674
  675.6 5.8 collective-permute-done.32
  (282 shorter events, 160.8 us)
Async XLA Ops:
  7.2 187.5 %all-gather.2.cloned.1.call-start = ((), (), s32[]{:S(2)}) async-start(), calls=%async_computation | async-start | bytes 17842176 | tf_op jit(solution)/shard_map/all_gather | solution.py:733
  10.4 510.0 %all-reduce.6.cloned.1.call-start = ((), (), s32[]{:S(2)}) async-start(), calls=%async_computation.1 | async-start | bytes 327680 | tf_op jit(solution)/shard_map/psum | solution.py:817
  17.8 18.5 %collective-permute-start.6 = (bf16[256,512]{1,0:T(8,128)(2,1)S(1)}, bf16[256,512]{1,0:T(8,128)(2,1)S(1)}, u32[]{:S(2)}, u32[]{:S(2)}) collective-permute-start(bf16[256,512]{1,0:T(8,128)(2,1)S(1)} %collective-permute-done.5), channel_id=1, source_target_pairs={{0,1},{1,2},{2,3},{3,0},{4,5},{5,6},{6,7},{7,4},{8,9},{9,10},{10,1... | collective-permute-start | bytes 786440 | tf_op jit(solution)/shard_map/ppermute | solution.py:653
  24.6 22.4 %collective-permute-start.1 = (bf16[272,512]{1,0:T(8,128)(2,1)S(1)}, bf16[272,512]{1,0:T(8,128)(2,1)S(1)}, u32[]{:S(2)}, u32[]{:S(2)}) collective-permute-start(bf16[272,512]{1,0:T(8,128)(2,1)S(1)} %collective-permute-done), channel_id=1, source_target_pairs={{0,1},{1,2},{2,3},{3,0},{4,5},{5,6},{6,7},{7,4},{8,9},{9,10},{10,1... | collective-permute-start | bytes 835592 | tf_op jit(solution)/shard_map/ppermute | solution.py:653
  47.1 17.3 %collective-permute-start.2 = (bf16[272,512]{1,0:T(8,128)(2,1)S(1)}, bf16[272,512]{1,0:T(8,128)(2,1)S(1)}, u32[]{:S(2)}, u32[]{:S(2)}) collective-permute-start(bf16[272,512]{1,0:T(8,128)(2,1)S(1)} %collective-permute-done.1), channel_id=1, source_target_pairs={{0,1},{1,2},{2,3},{3,0},{4,5},{5,6},{6,7},{7,4},{8,9},{9,10},{10,1... | collective-permute-start | bytes 835592 | tf_op jit(solution)/shard_map/ppermute | solution.py:653
  52.6 31.8 %collective-permute-start.8 = (bf16[4,256,512]{2,1,0:T(8,128)(2,1)S(1)}, bf16[4,256,512]{2,1,0:T(8,128)(2,1)}, u32[]{:S(2)}, u32[]{:S(2)}) collective-permute-start(bf16[4,256,512]{2,1,0:T(8,128)(2,1)S(1)} %bitcast_dynamic-update-slice_fusion.4), channel_id=1, source_target_pairs={{0,4},{4,0},{1,5},{5,1},{2,6},{6,2},{3,7},{7,3},{8,12},{12,8},{9,1... | collective-permute-start | bytes 3145736 | tf_op jit(solution)/shard_map/ppermute | solution.py:646
  64.4 59.9 %collective-permute-start.3 = (bf16[4,272,512]{2,1,0:T(8,128)(2,1)S(1)}, bf16[4,272,512]{2,1,0:T(8,128)(2,1)}, u32[]{:S(2)}, u32[]{:S(2)}) collective-permute-start(bf16[4,272,512]{2,1,0:T(8,128)(2,1)S(1)} %bitcast_dynamic-update-slice_fusion), channel_id=1, source_target_pairs={{0,4},{4,0},{1,5},{5,1},{2,6},{6,2},{3,7},{7,3},{8,12},{12,8},{9,1... | collective-permute-start | bytes 3342344 | tf_op jit(solution)/shard_map/ppermute | solution.py:646
  87.5 45.6 %collective-permute-start.9 = (bf16[2,4,256,512]{3,2,1,0:T(8,128)(2,1)}, bf16[2,4,256,512]{3,2,1,0:T(8,128)(2,1)}, u32[]{:S(2)}, u32[]{:S(2)}) collective-permute-start(bf16[2,4,256,512]{3,2,1,0:T(8,128)(2,1)} %pad_maximum_fusion.3), channel_id=1, source_target_pairs={{0,8},{8,0},{1,9},{9,1},{2,10},{10,2},{3,11},{11,3},{4,12},{12,4},... | collective-permute-start | bytes 6291464 | tf_op jit(solution)/shard_map/ppermute | solution.py:646
  286.4 76.7 %collective-permute-start.26 = (bf16[2,2,4,352,512]{4,3,2,1,0:T(8,128)(2,1)}, bf16[2,2,4,352,512]{4,3,2,1,0:T(8,128)(2,1)}, u32[]{:S(2)}, u32[]{:S(2)}) collective-permute-start(bf16[2,2,4,352,512]{4,3,2,1,0:T(8,128)(2,1)} %get-tuple-element.87), channel_id=1, source_target_pairs={{0,8},{8,0},{1,9},{9,1},{2,10},{10,2},{3,11},{11,3},{4,12},{12,4},... | collective-permute-start | bytes 17301512 | tf_op jit(solution)/shard_map/ppermute | solution.py:679
  313.3 41.4 %collective-permute-start.18 = (bf16[2,2,4,128,512]{4,3,2,1,0:T(8,128)(2,1)}, bf16[2,2,4,128,512]{4,3,2,1,0:T(8,128)(2,1)}, u32[]{:S(2)}, u32[]{:S(2)}) collective-permute-start(bf16[2,2,4,128,512]{4,3,2,1,0:T(8,128)(2,1)} %get-tuple-element.85), channel_id=1, source_target_pairs={{0,8},{8,0},{1,9},{9,1},{2,10},{10,2},{3,11},{11,3},{4,12},{12,4},... | collective-permute-start | bytes 6291464 | tf_op jit(solution)/shard_map/ppermute | solution.py:679
  354.2 176.2 %collective-permute-start.34 = (bf16[2,2,4,2,176,256]{5,4,3,2,1,0:T(8,128)(2,1)}, bf16[2,2,4,2,176,256]{5,4,3,2,1,0:T(8,128)(2,1)}, u32[]{:S(2)}, u32[]{:S(2)}) collective-permute-start(bf16[2,2,4,2,176,256]{5,4,3,2,1,0:T(8,128)(2,1)} %get-tuple-element.89), channel_id=1, source_target_pairs={{0,8},{8,0},{1,9},{9,1},{2,10},{10,2},{3,11},{11,3},{4,12},{12,4},... | collective-permute-start | bytes 8650760 | tf_op jit(solution)/shard_map/ppermute | solution.py:679
  358.4 166.2 %collective-permute-start.19 = (bf16[2,4,128,512]{3,2,1,0:T(8,128)(2,1)}, bf16[2,4,128,512]{3,2,1,0:T(8,128)(2,1)}, u32[]{:S(2)}, u32[]{:S(2)}) collective-permute-start(bf16[2,4,128,512]{3,2,1,0:T(8,128)(2,1)} %get-tuple-element.101), channel_id=1, source_target_pairs={{0,16},{16,0},{1,17},{17,1},{2,18},{18,2},{3,19},{19,3},{4,20},{20... | collective-permute-start | bytes 3145736 | tf_op jit(solution)/shard_map/ppermute | solution.py:674
  362.7 159.1 %collective-permute-start.11 = (bf16[2,4,128,512]{3,2,1,0:T(8,128)(2,1)}, bf16[2,4,128,512]{3,2,1,0:T(8,128)(2,1)}, u32[]{:S(2)}, u32[]{:S(2)}) collective-permute-start(bf16[2,4,128,512]{3,2,1,0:T(8,128)(2,1)} %get-tuple-element.103), channel_id=1, source_target_pairs={{0,16},{16,0},{1,17},{17,1},{2,18},{18,2},{3,19},{19,3},{4,20},{20... | collective-permute-start | bytes 3145736 | tf_op jit(solution)/shard_map/ppermute | solution.py:674
  371.8 199.5 %collective-permute-start.27 = (bf16[2,4,352,512]{3,2,1,0:T(8,128)(2,1)}, bf16[2,4,352,512]{3,2,1,0:T(8,128)(2,1)}, u32[]{:S(2)}, u32[]{:S(2)}) collective-permute-start(bf16[2,4,352,512]{3,2,1,0:T(8,128)(2,1)} %get-tuple-element.93), channel_id=1, source_target_pairs={{0,16},{16,0},{1,17},{17,1},{2,18},{18,2},{3,19},{19,3},{4,20},{20... | collective-permute-start | bytes 8650760 | tf_op jit(solution)/shard_map/ppermute | solution.py:674
  526.1 17.8 %collective-permute-start.20 = (bf16[4,128,512]{2,1,0:T(8,128)(2,1)S(1)}, bf16[4,128,512]{2,1,0:T(8,128)(2,1)S(1)}, u32[]{:S(2)}, u32[]{:S(2)}) collective-permute-start(bf16[4,128,512]{2,1,0:T(8,128)(2,1)S(1)} %get-tuple-element.114), channel_id=1, source_target_pairs={{0,4},{4,0},{1,5},{5,1},{2,6},{6,2},{3,7},{7,3},{8,12},{12,8},{9,1... | collective-permute-start | bytes 1572872 | tf_op jit(solution)/shard_map/ppermute | solution.py:674
  533.2 41.9 %collective-permute-start.35 = (bf16[2,4,2,176,256]{4,3,2,1,0:T(8,128)(2,1)S(1)}, bf16[2,4,2,176,256]{4,3,2,1,0:T(8,128)(2,1)S(1)}, u32[]{:S(2)}, u32[]{:S(2)}) collective-permute-start(bf16[2,4,2,176,256]{4,3,2,1,0:T(8,128)(2,1)S(1)} %get-tuple-element.95), channel_id=1, source_target_pairs={{0,16},{16,0},{1,17},{17,1},{2,18},{18,2},{3,19},{19,3},{4,20},{20... | collective-permute-start | bytes 4325384 | tf_op jit(solution)/shard_map/ppermute | solution.py:674
  534.4 16.9 %collective-permute-start.13 = (bf16[128,512]{1,0:T(8,128)(2,1)S(1)}, bf16[128,512]{1,0:T(8,128)(2,1)S(1)}, u32[]{:S(2)}, u32[]{:S(2)}) collective-permute-start(bf16[128,512]{1,0:T(8,128)(2,1)S(1)} %get-tuple-element.129), channel_id=1, source_target_pairs={{0,1},{1,2},{2,3},{3,0},{4,5},{5,6},{6,7},{7,4},{8,9},{9,10},{10,1... | collective-permute-start | bytes 393224 | tf_op jit(solution)/shard_map/ppermute | solution.py:674
  574.1 52.8 %collective-permute-start.28 = (bf16[4,352,512]{2,1,0:T(8,128)(2,1)S(1)}, bf16[4,352,512]{2,1,0:T(8,128)(2,1)S(1)}, u32[]{:S(2)}, u32[]{:S(2)}) collective-permute-start(bf16[4,352,512]{2,1,0:T(8,128)(2,1)S(1)} %get-tuple-element.97), channel_id=1, source_target_pairs={{0,4},{4,0},{1,5},{5,1},{2,6},{6,2},{3,7},{7,3},{8,12},{12,8},{9,1... | collective-permute-start | bytes 4325384 | tf_op jit(solution)/shard_map/ppermute | solution.py:674
  575.6 47.2 %collective-permute-start.36 = (bf16[4,2,176,256]{3,2,1,0:T(8,128)(2,1)S(1)}, bf16[4,2,176,256]{3,2,1,0:T(8,128)(2,1)S(1)}, u32[]{:S(2)}, u32[]{:S(2)}) collective-permute-start(bf16[4,2,176,256]{3,2,1,0:T(8,128)(2,1)S(1)} %get-tuple-element.107), channel_id=1, source_target_pairs={{0,4},{4,0},{1,5},{5,1},{2,6},{6,2},{3,7},{7,3},{8,12},{12,8},{9,1... | collective-permute-start | bytes 2162696 | tf_op jit(solution)/shard_map/ppermute | solution.py:674
  576.2 49.4 %collective-permute-start.25 = (bf16[2,128,512]{2,1,0:T(8,128)(2,1)S(1)}, bf16[2,128,512]{2,1,0:T(8,128)(2,1)S(1)}, u32[]{:S(2)}, u32[]{:S(2)}) collective-permute-start(bf16[2,128,512]{2,1,0:T(8,128)(2,1)S(1)} %pad_maximum_fusion.10), channel_id=1, source_target_pairs={{0,8},{8,0},{1,9},{9,1},{2,10},{10,2},{3,11},{11,3},{4,12},{12,4},... | collective-permute-start | bytes 786440 | tf_op jit(solution)/shard_map/ppermute | solution.py:646
  626.6 30.4 %collective-permute-start.39 = (bf16[2,176,256]{2,1,0:T(8,128)(2,1)S(1)}, bf16[2,176,256]{2,1,0:T(8,128)(2,1)S(1)}, u32[]{:S(2)}, u32[]{:S(2)}) collective-permute-start(bf16[2,176,256]{2,1,0:T(8,128)(2,1)S(1)} %get-tuple-element.120), channel_id=1, source_target_pairs={{0,3},{1,0},{2,1},{3,2},{4,7},{5,4},{6,5},{7,6},{8,11},{9,8},{10,9... | collective-permute-start | bytes 540680 | tf_op jit(solution)/shard_map/ppermute | solution.py:674
  627.2 36.2 %collective-permute-start.29 = (bf16[352,512]{1,0:T(8,128)(2,1)S(1)}, bf16[352,512]{1,0:T(8,128)(2,1)S(1)}, u32[]{:S(2)}, u32[]{:S(2)}) collective-permute-start(bf16[352,512]{1,0:T(8,128)(2,1)S(1)} %get-tuple-element.108), channel_id=1, source_target_pairs={{0,1},{1,2},{2,3},{3,0},{4,5},{5,6},{6,7},{7,4},{8,9},{9,10},{10,1... | collective-permute-start | bytes 1081352 | tf_op jit(solution)/shard_map/ppermute | solution.py:674
  628.4 42.7 %collective-permute-start.30 = (bf16[352,512]{1,0:T(8,128)(2,1)S(1)}, bf16[352,512]{1,0:T(8,128)(2,1)S(1)}, u32[]{:S(2)}, u32[]{:S(2)}) collective-permute-start(bf16[352,512]{1,0:T(8,128)(2,1)S(1)} %get-tuple-element.110), channel_id=1, source_target_pairs={{0,2},{1,3},{2,0},{3,1},{4,6},{5,7},{6,4},{7,5},{8,10},{9,11},{10,... | collective-permute-start | bytes 1081352 | tf_op jit(solution)/shard_map/ppermute | solution.py:674
  631.7 40.8 %collective-permute-start.31 = (bf16[352,512]{1,0:T(8,128)(2,1)S(1)}, bf16[352,512]{1,0:T(8,128)(2,1)S(1)}, u32[]{:S(2)}, u32[]{:S(2)}) collective-permute-start(bf16[352,512]{1,0:T(8,128)(2,1)S(1)} %get-tuple-element.109), channel_id=1, source_target_pairs={{0,3},{1,0},{2,1},{3,2},{4,7},{5,4},{6,5},{7,6},{8,11},{9,8},{10,9... | collective-permute-start | bytes 1081352 | tf_op jit(solution)/shard_map/ppermute | solution.py:674
  (75 other events, 812.5 us)
Sparse Core Ops, SparseCore 0:
  11.0 150.2 all-gather.1
  399.1 121.2 all-reduce.5

commit v2 on v1

--- a/solution.py
+++ b/solution.py
@@ -19,6 +19,7 @@
 FF = 2816
 HC = FF // 4
 TILE = 256
+FEED_TILE = 1024
 
 EPS = 1e-05
 HIGH = lax.Precision.HIGHEST
@@ -282,7 +283,7 @@
             struct((tokens, K), F32),
         ],
         compiler_params=params(32),
-        cost_estimate=cost(5e10, 20 * MIB),
+        cost_estimate=cost(1, 1),
         name="attend_back",
     )(segs.reshape(-1), q, k, v, logit, seg_c, seg_r, states, grad)
 
@@ -342,11 +343,15 @@
     out_ref, gn_ref, keep_gl, send_gl, keep_dn, send_dn, y_acc, hid, gate_g, lift_g,
 ):
     step = pl.program_id(0)
-    core = core_ref[0]
-
-    @pl.loop(0, n2_ref.shape[0] // TILE)
+
+    @pl.when(step == 0)
+    def _():
+        y_acc[...] = middle_ref[...]
+        gn_ref[...] = jnp.zeros_like(gn_ref)
+
+    @pl.loop(0, n2_ref.shape[0] // FEED_TILE)
     def _(t):
-        at = pl.ds(pl.multiple_of(t * TILE, TILE), TILE)
+        at = pl.ds(pl.multiple_of(t * FEED_TILE, FEED_TILE), FEED_TILE)
         gate = lift = back = None
         for r in range(2):
             n2 = n2_ref[at, r * 512 : (r + 1) * 512]
@@ -366,54 +371,33 @@
         gate_g[at, :] = grad_gate
         lift_g[at, :] = grad_lift
         for c in range(4):
-            part = dot(hidden, dn_ref[:, 0, c].reshape(HC, 256))
             lanes = slice(c * 256, (c + 1) * 256)
-
-            @pl.when(step == 0)
-            def _():
-                y_acc[at, lanes] = part
-
-            @pl.when(step > 0)
-            def _():
-                y_acc[at, lanes] += part
-
+            y_acc[at, lanes] += dot(hidden, dn_ref[:, 0, c].reshape(HC, 256))
         for r in range(2):
-            part = dot(grad_gate, gl_ref[:, r, 0, :176].reshape(HC, 512)) + dot(
+            lanes = slice(r * 512, (r + 1) * 512)
+            gn_ref[at, lanes] += dot(grad_gate, gl_ref[:, r, 0, :176].reshape(HC, 512)) + dot(
                 grad_lift, gl_ref[:, r, 0, 176:].reshape(HC, 512)
             )
-            lanes = slice(r * 512, (r + 1) * 512)
-
-            @pl.when(step == 0)
-            def _():
-                gn_ref[at, lanes] = part
-
-            @pl.when(step > 0)
-            def _():
-                gn_ref[at, lanes] += part
-
-        @pl.when(step == 3)
-        def _():
-            out_ref[at, :] = (middle_ref[at, :] + y_acc[at, :]).astype(BF16)
-
-    first = core == 0
-    for r in range(2):
-        n2 = n2_ref[:, r * 512 : (r + 1) * 512]
-        for m, source in enumerate((gate_g, lift_g)):
-            both = dot_tn(source[...], n2).astype(BF16)
-            low, high = both[: HC // 2], both[HC // 2 :]
-            mine = jnp.where(first, low, high)
-            other = jnp.where(first, high, low)
-            for x in range(2):
-                keep_gl[x, r, 0, m * 176 : (m + 1) * 176] = mine[x * 176 : (x + 1) * 176]
-                send_gl[x, r, 0, m * 176 : (m + 1) * 176] = other[x * 176 : (x + 1) * 176]
-    for c in range(4):
-        both = dot_tn(hid[...], dy_ref[:, c * 256 : (c + 1) * 256]).astype(BF16)
+
+    @pl.when(step == 3)
+    def _():
+        out_ref[...] = y_acc[...].astype(BF16)
+
+    first = core_ref[0] == 0
+    for m, (source, right) in enumerate(((gate_g, n2_ref), (lift_g, n2_ref), (hid, dy_ref))):
+        both = dot_tn(source[...], right[...]).astype(BF16)
         low, high = both[: HC // 2], both[HC // 2 :]
         mine = jnp.where(first, low, high)
         other = jnp.where(first, high, low)
-        for x in range(2):
-            keep_dn[x, 0, c, 0] = mine[x * 176 : (x + 1) * 176]
-            send_dn[x, 0, c, 0] = other[x * 176 : (x + 1) * 176]
+        for part, gl_out, dn_out in ((mine, keep_gl, keep_dn), (other, send_gl, send_dn)):
+            for x in range(2):
+                piece = part[x * 176 : (x + 1) * 176]
+                if m < 2:
+                    for r in range(2):
+                        gl_out[x, r, 0, m * 176 : (m + 1) * 176] = piece[:, r * 512 : (r + 1) * 512]
+                else:
+                    for c in range(4):
+                        dn_out[x, 0, c, 0] = piece[:, c * 256 : (c + 1) * 256]
 
 
 def feed(core, n2, dy, middle, weights):
@@ -530,7 +514,7 @@
     )(grad, middle, dy, og, mixed, weights, head_gain, gain_two)
 
 
-def weight_grad_kernel(plan, core_ref, *refs):
+def weight_grad_kernel(plan, row_first, core_ref, *refs):
     count = 2 * len(plan)
     keep_ref, send_ref = refs[-2:]
     lefts, rights = refs[:count], refs[count:-2]
@@ -540,10 +524,11 @@
             for ref, left in ((keep_ref, lefts[2 * lefts_at]), (send_ref, lefts[2 * lefts_at + 1])):
                 part = dot_tn(left[...], right).astype(BF16)
                 for x in range(2):
-                    ref[x, 0, 0, :, start : start + width] = part[x * 128 : (x + 1) * 128]
-
-
-def weight_grads(core, lefts, rights, plan):
+                    at = (0, x, 0) if row_first else (x, 0, 0)
+                    ref[(*at, slice(None), slice(start, start + width))] = part[x * 128 : (x + 1) * 128]
+
+
+def weight_grads(core, lefts, rights, plan, row_first=False):
     tokens = lefts[0].shape[0]
     specs = []
     for left in lefts:
@@ -551,16 +536,19 @@
         specs.append(pl.BlockSpec((tokens, 256), lambda r, c, core: (0, r * 2 + 1 - core[0])))
     for right in rights:
         specs.append(pl.BlockSpec((tokens, right.shape[1] // 4), lambda r, c, core: (0, c)))
-    out = pl.BlockSpec((2, 1, 1, 128, 512), lambda r, c, core: (0, r, c, 0, 0))
+    if row_first:
+        out = pl.BlockSpec((1, 2, 1, 128, 512), lambda r, c, core: (r, 0, c, 0, 0))
+    else:
+        out = pl.BlockSpec((2, 1, 1, 128, 512), lambda r, c, core: (0, r, c, 0, 0))
     operands = [left for left in lefts for _ in range(2)] + list(rights)
     return pl.pallas_call(
-        functools.partial(weight_grad_kernel, plan),
+        functools.partial(weight_grad_kernel, plan, row_first),
         grid_spec=pltpu.PrefetchScalarGridSpec(
             num_scalar_prefetch=1, grid=(2, 4), in_specs=specs, out_specs=[out, out]
         ),
         out_shape=[struct((2, 2, 4, 128, 512), BF16)] * 2,
         compiler_params=params(40),
-        cost_estimate=cost(2 * tokens * D * 2048, 12 * MIB),
+        cost_estimate=cost(1, 1),
         name="weight_grads",
     )(core, *operands)
 
@@ -635,24 +623,64 @@
             struct((1, D), F32),
         ],
         compiler_params=params(56),
-        cost_estimate=cost(2 * tokens * D * 3072, 30 * MIB),
+        cost_estimate=cost(2 * tokens * D * 3072, 100 * MIB),
         name="unproject",
     )(x, normed, gq, gk, gv, glog, logit, low, gog, gm, weights, out_weights, ddt, du, gain)
 
 
+def fold_kernel(place_ref, keep_gl, got_gl, keep_dn, got_dn, go_g, st_g, go_l, st_l, *downs):
+    i = pl.program_id(0)
+    x_at, row_at = place_ref[0], place_ref[1]
+
+    def both(left, right):
+        return (left.astype(F32) + right.astype(F32)).astype(BF16)
+
+    for r in range(2):
+        for ref, x in ((go_g, 1 - x_at), (st_g, x_at)):
+            ref[0, r] = both(keep_gl[x, r, 0, :176], got_gl[x, r, 0, :176])
+    for x in range(2):
+        for ref, r in ((go_l, 1 - row_at), (st_l, row_at)):
+            ref[0, x] = both(keep_gl[x, r, 0, 176:], got_gl[x, r, 0, 176:])
+    for shift in range(4):
+
+        @pl.when(i == shift)
+        def _():
+            downs[shift][...] = both(keep_dn[:, :, 0], got_dn[:, :, 0])
+
+
+def fold(place, keep_gl, got_gl, keep_dn, got_dn):
+    gl = pl.BlockSpec((2, 2, 1, 352, 512), lambda i, p: (0, 0, i, 0, 0))
+    dn = pl.BlockSpec((2, 2, 1, 2, 176, 256), lambda i, p: (0, 0, lax.rem(p[2] + i, 4), 0, 0, 0))
+    out = pl.BlockSpec((1, 2, 176, 512), lambda i, p: (i, 0, 0, 0))
+    down = pl.BlockSpec((2, 2, 2, 176, 256), lambda i, p: (0, 0, 0, 0, 0))
+    return pl.pallas_call(
+        fold_kernel,
+        grid_spec=pltpu.PrefetchScalarGridSpec(
+            num_scalar_prefetch=1,
+            grid=(4,),
+            in_specs=[gl, gl, dn, dn],
+            out_specs=[out] * 4 + [down] * 4,
+        ),
+        out_shape=[struct((4, 2, 176, 512), BF16)] * 4 + [struct((2, 2, 2, 176, 256), BF16)] * 4,
+        compiler_params=params(48),
+        cost_estimate=cost(1, 26 * MIB),
+        name="fold",
+    )(place, keep_gl, got_gl, keep_dn, got_dn)
+
+
+def placed(parts, axis):
+    me, count = lax.axis_index(axis), len(parts)
+    whole = jnp.zeros((count,) + parts[0].shape, parts[0].dtype)
+    for shift, part in enumerate(parts):
+        whole = lax.dynamic_update_index_in_dim(whole, part, lax.rem(me + count - shift, count), 0)
+    return whole
+
+
 def ring_gather(part, axis, count):
-    me = lax.axis_index(axis)
-    if count == 2:
-        other = lax.ppermute(part, axis, [(0, 1), (1, 0)])
-        first = me == 0
-        return jnp.stack([jnp.where(first, part, other), jnp.where(first, other, part)])
-    whole = jnp.zeros((count,) + part.shape, part.dtype)
-    whole = lax.dynamic_update_index_in_dim(whole, part, me, 0)
-    moving = part
-    for step in range(1, count):
-        moving = lax.ppermute(moving, axis, [(i, (i + 1) % count) for i in range(count)])
-        whole = lax.dynamic_update_index_in_dim(whole, moving, lax.rem(me + count - step, count), 0)
-    return whole
+    parts = [part]
+    for _ in range(1, count):
+        parts.append(lax.ppermute(parts[-1], axis, [(i, (i + 1) % count) for i in range(count)]))
+    return placed(parts, axis)
 
 
 def added(parts):
@@ -662,26 +690,38 @@
     return total.astype(BF16)
 
 
-def scatter_add(arrays, axis, count):
-    me = lax.axis_index(axis)
-
-    def piece(place):
-        return added([lax.dynamic_index_in_dim(array, place, 0, keepdims=False) for array in arrays])
-
-    received = []
-    for shift in range(1, count):
-        going = piece(lax.rem(me + shift, count))
-        received.append(lax.ppermute(going, axis, [(i, (i + shift) % count) for i in range(count)]))
-    return [piece(me)] + received
-
-
-def reduce_pack(keep, send, rows_count, cols_count):
-    arrays = [keep, lax.ppermute(send, "core", [(0, 1), (1, 0)])]
-    arrays = scatter_add(arrays, "x", 2)
-    arrays = scatter_add(arrays, "row", rows_count)
-    arrays = scatter_add(arrays, "col", cols_count)
-    total = added(arrays)
-    return ring_gather(ring_gather(total, "x", 2), "core", 2)
+def tied(*groups):
+    flat, tree = jax.tree.flatten(groups)
+    return jax.tree.unflatten(tree, lax.optimization_barrier(flat))
+
+
+def swap(part, axis, bit=1):
+    return lax.ppermute(part, axis, [(i, i ^ bit) for i in range(lax.axis_size(axis))])
+
+
+def piece_of(arrays, place, dim):
+    return added([lax.dynamic_index_in_dim(array, place, dim, keepdims=False) for array in arrays])
+
+
+def going(arrays, axis, dim):
+    me, count = lax.axis_index(axis), lax.axis_size(axis)
+    return [piece_of(arrays, lax.rem(me + shift, count), dim) for shift in range(1, count)]
+
+
+def send(pieces, axis):
+    count = lax.axis_size(axis)
+    return [
+        lax.ppermute(piece, axis, [(i, (i + shift) % count) for i in range(count)])
+        for shift, piece in enumerate(pieces, 1)
+    ]
+
+
+def staying(arrays, axis, dim):
+    return piece_of(arrays, lax.axis_index(axis), dim)
+
+
+def share(part):
+    return ring_gather(ring_gather(part, "x", 2), "core", 2)
 
 
 def small_block(ddt, du, bias, g1, hg, g2):
@@ -714,7 +754,6 @@
     fast = row_count == 2 and col_count == 4 and lax.axis_size("x") == 2
     core = lax.axis_index("core")
     quarter = lax.axis_index("x") * 2 + core
-    owned = (query_weight, key_weight, value_weight, outgate_weight, out_weight)
 
     if fast:
         feed_rows = jnp.concatenate(
@@ -732,16 +771,15 @@
         )
         feed_full = lax.all_gather(feed_rows, AXES, axis=0, tiled=True).reshape(4, 2, 4, 352, 768)
 
-        def gather(part):
-            part = ring_gather(ring_gather(part, "col", col_count), "row", row_count)
-            return ring_gather(part, "core", 2)
-
         qkv = jnp.concatenate([query_weight, key_weight, value_weight], axis=1)
         qkv = lax.dynamic_slice_in_dim(qkv, core * 256, 256, 0)
         small = small_block(decay_down.T, decay_up, decay_bias, norm1_gain, head_gain, norm2_gain)
-        qkv_full = gather(jnp.concatenate([qkv, small], axis=0))
+        by_col = ring_gather(jnp.concatenate([qkv, small], axis=0), "col", col_count)
         ogout = jnp.concatenate([outgate_weight, out_weight], axis=1)
-        ogout_full = gather(lax.dynamic_slice_in_dim(ogout, core * 256, 256, 0))
+        ogout = lax.dynamic_slice_in_dim(ogout, core * 256, 256, 0)
+        ogout, by_col = tied(ogout, by_col)
+        ogout_cols = [ogout, *send([ogout] * (col_count - 1), "col")]
+        qkv_full = ring_gather(ring_gather(by_col, "row", row_count), "core", 2)
         small = qkv_full[0, :, :, 256:]
         ddt = small[:, :, :4].reshape(2, LOW, 512)
         du = small[:, :, 4:12, :HK].transpose(0, 2, 1, 3).reshape(LOW, K)
@@ -784,7 +822,15 @@
     core_at = (core if fast else jnp.zeros_like(core)).astype(jnp.int32).reshape(1)
 
     normed, q, k, v, low, logit = project(layer_input, g1, qkv_full, ddt, du, bias)
+    if fast:
+        q, ogout_cols = tied(q, ogout_cols)
+        ogout = placed(ogout_cols, "col")
+        other_row = swap(ogout, "row")
     mixed, states = attend(q, k, v, logit, segment_ids, seg_c, seg_r)
+    if fast:
+        mixed, other_row = tied(mixed, other_row)
+        ogout = placed([ogout, other_row], "row")
+        ogout_full = placed([ogout, swap(ogout, "core")], "core")
     og, gated, middle, normed_two = mix(layer_input, normed, mixed, ogout_full, hg, g2)
     layer_output, grad_normed_two, keep_gl, send_gl, keep_dn, send_dn = feed(
         core_at, normed_two, cotangent, middle, feed_full
@@ -792,60 +838,126 @@
     grad_middle, branch, grad_og, grad_mixed, grad_g2, grad_hg = unmix(
         grad_normed_two, middle, cotangent, og, mixed, ogout_full, hg, g2
     )
+    if fast:
+        got_gl, got_dn = swap(send_gl, "core"), swap(send_dn, "core")
+        x_at, row_at = lax.axis_index("x"), lax.axis_index("row")
+        place = jnp.stack([x_at, row_at, lax.axis_index("col")]).astype(jnp.int32)
+        go_g, st_g, go_l, st_l, st_d, *go_d = fold(place, keep_gl, got_gl, keep_dn, got_dn)
+        branch, grad_og, go_g, go_l, go_d = tied(branch, grad_og, go_g, go_l, go_d)
+        got_g, got_l, got_d = swap(go_g, "x"), swap(go_l, "row"), send(go_d, "col")
     keep_oo, send_oo = weight_grads(
-        core_at, [normed, gated], [grad_og, branch], ((0, ((0, 0, 256),)), (1, ((256, 1, 256),)))
-    )
+        core_at, [normed, gated], [grad_og, branch], ((0, ((0, 0, 256),)), (1, ((256, 1, 256),))), True
+    )
+    if fast:
+        grad_mixed, send_oo = tied(grad_mixed, send_oo)
+        got_oo = swap(send_oo, "core")
     gq, gk, gv, glog = attend_back(q, k, v, logit, segment_ids, seg_c, seg_r, states, grad_mixed)
     keep_qkv, send_qkv = weight_grads(
         core_at, [normed], [gq, gk, gv], ((0, ((0, 0, 128), (128, 1, 128), (256, 2, 256))),)
     )
+    if fast:
+        send_qkv, got_g, got_l, got_d = tied(send_qkv, got_g, got_l, got_d)
+        got_qkv = swap(send_qkv, "core")
+        gate, lift, down = [st_g, got_g], [st_l, got_l], [st_d, *got_d]
+        both = [jnp.concatenate(parts, axis=1) for parts in zip(gate, lift)]
+        both = [part.reshape(2, 2, *part.shape[1:]) for part in both]
+        col_hi, col_lo = lax.axis_index("col") // 2, lax.axis_index("col") % 2
+        go_gl, go_d = piece_of(both, 1 - col_lo, 1), piece_of(down, 1 - x_at, 0)
+        go_qkv = piece_of([keep_qkv, got_qkv], 1 - x_at, 0)
+        go_oo = piece_of([keep_oo, got_oo], 1 - row_at, 0)
+        glog, go_gl, go_d, go_qkv, go_oo = tied(glog, go_gl, go_d, go_qkv, go_oo)
+        got_gl, got_d = swap(go_gl, "col"), swap(go_d, "x")
+        got_qkv_x, got_oo_r = swap(go_qkv, "x"), swap(go_oo, "row")
     input_grad, grad_ddt, grad_du, grad_bias, grad_g1 = unproject(
         layer_input, normed, gq, gk, gv, glog, logit, low, grad_og, grad_middle, qkv_full, ogout_full, ddt, du, g1
     )
 
-    tiny = jnp.concatenate(
-        [
-            grad_ddt,
-            jnp.pad(grad_du, ((0, 0), (0, D - K))),
-            jnp.concatenate([grad_bias, grad_hg, jnp.zeros((1, D - K - HV), F32)], axis=1),
-            grad_g1,
-            grad_g2,
-            jnp.zeros((5, D), F32),
-        ],
-        axis=0,
-    )
-    tiny = lax.psum(tiny, AXES)
-    r, c = lax.axis_index("row"), lax.axis_index("col")
-
-    def own(line, size):
-        return lax.dynamic_slice_in_dim(line, (r * col_count + c) * size, size, 0)
-
-    def own_block(full, shape):
-        return lax.dynamic_slice(full, (r * shape[0], c * shape[1]), shape)
-
-    out_bias = own(tiny[32, :K], decay_bias.shape[0])
-    out_hg = own(tiny[32, K : K + HV], head_gain.shape[0])
-    out_g1 = own(tiny[33], norm1_gain.shape[0])
-    out_g2 = own(tiny[34], norm2_gain.shape[0])
-    out_du = own_block(tiny[16:32, :K], decay_up.shape)
-    down_rows = decay_down.shape
-    out_dd = lax.dynamic_slice(tiny, (c * down_rows[1], r * down_rows[0]), down_rows[::-1]).T
-
     if fast:
-        gl = reduce_pack(keep_gl, send_gl, row_count, col_count)
-        dn = reduce_pack(keep_dn, send_dn, row_count, col_count)
-        oo = reduce_pack(keep_oo, send_oo, row_count, col_count)
-        qkv = reduce_pack(keep_qkv, send_qkv, row_count, col_count)
-        gl = gl.reshape(2, 2, 2, 176, 512).transpose(2, 0, 1, 3, 4).reshape(2, HC, 512)
-        out_gate, out_lift = gl[0].T, gl[1].T
-        out_down = dn.transpose(2, 0, 1, 3, 4).reshape(1408, 256)
-        oo = oo.reshape(512, 512)
-        qkv = qkv.reshape(512, 512)
+        late = (got_gl, got_d, got_oo_r, got_qkv_x)
+        input_grad, grad_g1, late = tied(input_grad, grad_g1, late)
+        got_gl, got_d, got_oo_r, got_qkv_x = late
+        qkv = [piece_of([keep_qkv, got_qkv], x_at, 0), got_qkv_x]
+        oo = [piece_of([keep_oo, got_oo], row_at, 0), got_oo_r]
+        both = [piece_of(both, col_lo, 1), got_gl]
+        go_qkv, go_oo, go_gl = piece_of(qkv, 1 - row_at, 0), piece_of(oo, 1 - x_at, 0), piece_of(both, 1 - col_hi, 0)
+        go_qkv, go_oo, go_gl, grad_g1 = tied(go_qkv, go_oo, go_gl, grad_g1)
+        qkv = [piece_of(qkv, row_at, 0), swap(go_qkv, "row")]
+        oo = [piece_of(oo, x_at, 0), swap(go_oo, "x")]
+        both = [piece_of(both, col_hi, 0), swap(go_gl, "col", 2)]
+        tiny = jnp.concatenate(
+            [
+                grad_ddt.reshape(4, 4, 2, 512).transpose(2, 0, 1, 3),
+                jnp.pad(grad_du.reshape(2, 8, 4, HK).transpose(0, 2, 1, 3), ((0, 0), (0, 0), (0, 0), (0, 384))),
+                jnp.concatenate(
+                    [
+                        jnp.pad(grad_bias.reshape(2, 4, 64), ((0, 0), (0, 0), (0, 64))),
+                        grad_g1.reshape(2, 4, 128),
+                        jnp.pad(grad_hg.reshape(2, 4, 32), ((0, 0), (0, 0), (0, 96))),
+                        grad_g2.reshape(2, 4, 128),
+                    ],
+                    axis=-1,
+                ).reshape(2, 4, 1, 512),
+                jnp.zeros((2, 4, 3, 512), F32),
+            ],
+            axis=2,
+        )
+        tiny = tiny + swap(tiny, "core")
+        tiny = tiny + swap(tiny, "x")
+        tiny = added([staying([tiny], "row", 0), *send(going([tiny], "row", 0), "row")])
+        gate, lift = [[part[at : at + 2] for part in both] for at in (0, 2)]
+        down = [piece_of(down, x_at, 0), got_d]
+        gate = [piece_of(gate, row_at, 0), swap(piece_of(gate, 1 - row_at, 0), "row")]
+        down = [piece_of(down, row_at, 0), swap(piece_of(down, 1 - row_at, 0), "row")]
+        lift = [piece_of(lift, x_at, 0), swap(piece_of(lift, 1 - x_at, 0), "x")]
+        down = added(down)
+        feeds = share(jnp.concatenate([added(gate), added(lift), down[0], down[1]], axis=-1))
+        rest = jnp.concatenate([added(qkv), added(oo)], axis=-1)
+        rest = share(added([staying([rest], "col", 0), *send(going([rest], "col", 0), "col")]))
+        tiny = added([staying([tiny], "col", 0), *send(going([tiny], "col", 0), "col")]).astype(F32)
+        out_dd, out_du = tiny[:4].T, tiny[4:12, :HK]
+        out_bias, out_g1, out_hg, out_g2 = tiny[12, :64], tiny[12, 128:256], tiny[12, 256:288], tiny[12, 384:]
+    else:
+        tiny = jnp.concatenate(
+            [
+                grad_ddt,
+                jnp.pad(grad_du, ((0, 0), (0, D - K))),
+                jnp.concatenate([grad_bias, grad_hg, jnp.zeros((1, D - K - HV), F32)], axis=1),
+                grad_g1,
+                grad_g2,
+                jnp.zeros((5, D), F32),
+            ],
+            axis=0,
+        )
+        tiny = lax.psum(tiny, AXES)
+        r, c = lax.axis_index("row"), lax.axis_index("col")
+
+        def own(line, size):
+            return lax.dynamic_slice_in_dim(line, (r * col_count + c) * size, size, 0)
+
+        def own_block(full, shape):
+            return lax.dynamic_slice(full, (r * shape[0], c * shape[1]), shape)
+
+        out_bias = own(tiny[32, :K], decay_bias.shape[0])
+        out_hg = own(tiny[32, K : K + HV], head_gain.shape[0])
+        out_g1 = own(tiny[33], norm1_gain.shape[0])
+        out_g2 = own(tiny[34], norm2_gain.shape[0])
+        out_du = own_block(tiny[16:32, :K], decay_up.shape)
+        down_rows = decay_down.shape
+        out_dd = lax.dynamic_slice(tiny, (c * down_rows[1], r * down_rows[0]), down_rows[::-1]).T
+
+    if fast:
+        out_gate = feeds[..., :512].reshape(HC, 512).T
+        out_lift = feeds[..., 512:1024].reshape(HC, 512).T
+        out_down = jnp.stack([feeds[..., 1024:1280], feeds[..., 1280:]]).reshape(1408, 256)
+        qkv = rest[..., :512].reshape(512, 512)
+        oo = rest[..., 512:].reshape(512, 512)
         shards = [qkv[:, :128], qkv[:, 128:256], qkv[:, 256:], oo[:, :256], oo[:, 256:], out_gate, out_lift, out_down]
     else:
 
         def joined(keep, send):
             return jnp.stack([keep, send])
+
+        keep_oo, send_oo = keep_oo.swapaxes(0, 1), send_oo.swapaxes(0, 1)
 
         def matrix(pack):
             return pack.transpose(2, 0, 1, 4, 3, 5).reshape(D, -1)

time: 701 us -> 508 us (0.72)
  waiting for transfers between devices: 319 us -> 146 us
  other arithmetic: 54.2 us -> 36.2 us
  local copies, waits for them, and re-layouts: 34.6 us -> 46.5 us
  starting transfers between devices: 64.5 us -> 54.2 us
    psum x1 -> x0, waiting for transfers between devices: 121 us -> none  [per_device(): tiny = lax.psum(tiny, AXES)]
    ppermute x42, waiting for transfers between devices: 197 us -> 146 us  [the longest x9 72.1 us: ring_gather(): lax.ppermute(parts[-1], axis, [(i, (i + 1) % count) for i in range(count)])]
    another operation x21 -> x3, other arithmetic: 20.4 us -> 3.81 us  [ring_gather(): jnp.stack([jnp.where(first, part, other), jnp.where(first, other, part)])]
    pallas_call x1, Pallas kernels: 91.7 us -> 79.3 us  [feed(): pl.pallas_call(feed_kernel, grid_spec=pltpu.PrefetchScalarGridSpec(num_sc...]
    dynamic_update_slice x7 -> x22, local copies, waits for them, and re-layouts: 0.16 us -> 11.4 us  [placed(): lax.dynamic_update_index_in_dim(whole, part, lax.rem(me + count - shift,...]
    pallas_call x2 -> x3, Pallas kernels: 20 us -> 30.7 us  [the longest x2 20 us: weight_grads(): pl.pallas_call(functools.partial(weight_grad_kernel, plan, row_first), gr...]
    ppermute x42, starting transfers between devices: 64.4 us -> 54.1 us  [the longest x20 26.8 us: swap(): lax.ppermute(part, axis, [(i, i ^ bit) for i in range(lax.axis_size(axis))])]
    convert_element_type x16, other arithmetic: 25.7 us -> 17.9 us  [added(): return total.astype(BF16)]
  transfers between devices with their start and end apart: 44 -> 43, of which waited for: 20 -> 21; matrix products, arithmetic and copies ran while one was open for 9% -> 9% of each run, Pallas kernels for 17% -> 23%
where the time goes in v2:
time: 508 us; the launch traced here: 506 us
  Pallas kernels  207 us (41%)
  waiting for transfers between devices  146 us (29%)
  starting transfers between devices  54.2 us (11%)
  local copies, waits for them, and re-layouts  46.5 us (9%)
  other arithmetic  36.2 us (7%)
  between operations  15.5 us (3%)
    pallas_call x1, Pallas kernels, feed(): pl.pallas_call(feed_kernel, grid_spec=pltpu.PrefetchScalarGridSpec(num_sc...  79.3 us
    ppermute x9, waiting for transfers between devices, ring_gather(): lax.ppermute(parts[-1], axis, [(i, (i + 1) % count) for i in range(count)])  72.1 us
    ppermute x13, waiting for transfers between devices, send(): lax.ppermute(piece, axis, [(i, (i + shift) % count) for i in range(count)])  45.6 us
    ppermute x20, waiting for transfers between devices, swap(): lax.ppermute(part, axis, [(i, i ^ bit) for i in range(lax.axis_size(axis))])  28.8 us
    ppermute x20, starting transfers between devices, swap(): lax.ppermute(part, axis, [(i, i ^ bit) for i in range(lax.axis_size(axis))])  26.8 us
    unnamed x127, local copies, waits for them, and re-layouts  25.3 us
    pallas_call x1, Pallas kernels, attend_back(): pl.pallas_call(functools.partial(attend_back_kernel, spans), grid_spec=pl...  24.5 us
    pallas_call x1, Pallas kernels, unproject(): pl.pallas_call(unproject_kernel, grid=(tokens // TILE,), in_specs=[rows(T...  20.9 us
  transfers between devices with their start and end apart: 43, of which 21 were waited for; matrix products, arithmetic and copies ran while one was open for 9% of the time, Pallas kernels for 23%

profile of v2, /device:TPU:9, one launch (start us, length us, event | category | flops | bytes accessed | tf_op | source)
XLA Modules:
  0.0 505.7 jit_solution(5428989098766388429)
XLA Ops:
  12.0 6.2 %collective-permute-done = bf16[272,512]{1,0:T(8,128)(2,1)S(1)} collective-permute-done((bf16[272,512]{1,0:T(8,128)(2,1)S(1)}, bf16[272,512]{1,0:T(8,128)(2,1)S(1)}, u32[]{:S(2)}, u32[]{:S(2)}) %collective-permute-start) | collective-permute-done | bytes 278560 | tf_op jit(solution)/shard_map/ppermute | solution.py:682
  19.7 9.4 %collective-permute-done.1 = bf16[272,512]{1,0:T(8,128)(2,1)S(1)} collective-permute-done((bf16[272,512]{1,0:T(8,128)(2,1)S(1)}, bf16[272,512]{1,0:T(8,128)(2,1)S(1)}, u32[]{:S(2)}, u32[]{:S(2)}) %collective-permute-start.1) | collective-permute-done | bytes 278560 | tf_op jit(solution)/shard_map/ppermute | solution.py:682
  29.2 13.7 %collective-permute-done.2 = bf16[272,512]{1,0:T(8,128)(2,1)S(1)} collective-permute-done((bf16[272,512]{1,0:T(8,128)(2,1)S(1)}, bf16[272,512]{1,0:T(8,128)(2,1)S(1)}, u32[]{:S(2)}, u32[]{:S(2)}) %collective-permute-start.2) | collective-permute-done | bytes 278560 | tf_op jit(solution)/shard_map/ppermute | solution.py:682
  45.9 28.1 %collective-permute-done.3 = bf16[4,272,512]{2,1,0:T(8,128)(2,1)S(1)} collective-permute-done((bf16[4,272,512]{2,1,0:T(8,128)(2,1)S(1)}, bf16[4,272,512]{2,1,0:T(8,128)(2,1)S(1)}, u32[]{:S(2)}, u32[]{:S(2)}) %collective-permute-start.3) | collective-permute-done | bytes 1114144 | tf_op jit(solution)/shard_map/ppermute | solution.py:682
  80.3 5.2 %collective-permute-start.6 = (bf16[256,512]{1,0:T(8,128)(2,1)S(1)}, bf16[256,512]{1,0:T(8,128)(2,1)}, u32[]{:S(2)}, u32[]{:S(2)}) collective-permute-start(bf16[256,512]{1,0:T(8,128)(2,1)S(1)} %fusion.31), channel_id=1, source_target_pairs={{0,2},{1,3},{2,0},{3,1},{4,6},{5,7},{6,4},{7,5},{8,10},{9,11},{10,... | collective-permute-start | bytes 786440 | tf_op jit(solution)/shard_map/ppermute | solution.py:714
  92.8 10.2 %project.1 = (bf16[1024,1024]{1,0:T(8,128)(2,1)S(1)}, bf16[1024,512]{1,0:T(8,128)(2,1)S(1)}, bf16[1024,512]{1,0:T(8,128)(2,1)S(1)}, bf16[1024,1024]{1,0:T(8,128)...) custom-call(bf16[1024,1024]{1,0:T(8,128)(2,1)S(1)} %copy-done.15, f32[1,1024]{1,0:T(1,128)S(1)} %convert.38.gain_ref.g1_ref, ...), custom_call_target="tpu_custom_call" | custom-call | flops 4294967296 | bytes 14680064 | tf_op jit(solution)/shard_map/project/pallas_call | solution.py:90
  104.5 14.9 %collective-permute-done.6 = bf16[256,512]{1,0:T(8,128)(2,1)} collective-permute-done((bf16[256,512]{1,0:T(8,128)(2,1)S(1)}, bf16[256,512]{1,0:T(8,128)(2,1)}, u32[]{:S(2)}, u32[]{:S(2)}) %collective-permute-start.6) | collective-permute-done | bytes 262176 | tf_op jit(solution)/shard_map/ppermute | solution.py:714
  119.4 14.1 %collective-permute-done.7 = bf16[256,512]{1,0:T(8,128)(2,1)} collective-permute-done((bf16[256,512]{1,0:T(8,128)(2,1)S(1)}, bf16[256,512]{1,0:T(8,128)(2,1)}, u32[]{:S(2)}, u32[]{:S(2)}) %collective-permute-start.7) | collective-permute-done | bytes 262176 | tf_op jit(solution)/shard_map/ppermute | solution.py:714
  136.0 14.4 %attend.1 = (f32[1024,1024]{1,0:T(8,128)S(1)}, bf16[16,4,256,128]{3,2,1,0:T(8,128)(2,1)S(1)}) custom-call(s32[1024]{0:T(1024)S(1)} %bitcast.231, bf16[1024,512]{1,0:T(8,128)(2,1)S(1)} %get-tuple-element.104.q_ref, bf16[1024,512]{1,0:T(8,128)(2,1)S(1)} %get-tuple-element.105.k_ref, bf16[1024,1024]{1,0:T(8,128)(2,1)S(1)} %get-tuple-element.106.v_ref, ...), custom_call_target="tpu_custom_call" | custom-call | flops 20000000000 | bytes 16777216 | tf_op jit(solution)/shard_map/attend/pallas_call | solution.py:176
  154.4 4.4 collective-permute-done.8
  169.1 12.6 %mix.1 = (f32[1024,1024]{1,0:T(8,128)}, bf16[1024,1024]{1,0:T(8,128)(2,1)S(1)}, f32[1024,1024]{1,0:T(8,128)}, bf16[1024,1024]{1,0:T(8,128)(2,1)S(1)}) custom-call(bf16[1024,1024]{1,0:T(8,128)(2,1)} %x_ref.5, bf16[1024,1024]{1,0:T(8,128)(2,1)} %copy-done.2, f32[1024,1024]{1,0:T(8,128)} %copy-done.10, bf16[2,2,4,256,512]{4,3,2,1,0:T(8,128)(2,1)} %copy-done.39, ...), custom_call_target="tpu_custom_call" | custom-call | flops 4294967296 | bytes 25165824 | tf_op jit(solution)/shard_map/mix/pallas_call | solution.py:317
  184.4 79.3 %feed.1 = (bf16[1024,1024]{1,0:T(8,128)(2,1)}, f32[1024,1024]{1,0:T(8,128)}, bf16[2,2,4,352,512]{4,3,2,1,0:T(8,128)(2,1)}, bf16[2,2,4,352,512]{4,3,2,1,0:T(8,128...) custom-call(s32[1]{0:T(128)} %bitcast.core_ref, ...), custom_call_target="tpu_custom_call" | custom-call | flops 53150220288 | bytes 62914560 | tf_op jit(solution)/shard_map/feed/pallas_call | solution.py:408
  264.4 14.2 %unmix.1 = (f32[1024,1024]{1,0:T(8,128)}, bf16[1024,1024]{1,0:T(8,128)(2,1)}, bf16[1024,1024]{1,0:T(8,128)(2,1)}, bf16[1024,1024]{1,0:T(8,128)(2,1)}, f32[1,1024]{1,0:T(1,128)}, /*index=5*/f32[1,256]{1,0:T(1,128)}) custom-call(f32[1024,1024]{1,0:T(8,128)} %get-tuple-element.119.gn_ref, f32[1024,1024]{1,0:T(8,128)} %get-tuple-element.116.middle_ref, ...), custom_call_target="tpu_custom_call" | custom-call | flops 2147483648 | bytes 31457280 | tf_op jit(solution)/shard_map/unmix/pallas_call | solution.py:489
  281.1 10.8 %fold.1 = (bf16[4,2,176,512]{3,2,1,0:T(8,128)(2,1)}, bf16[4,2,176,512]{3,2,1,0:T(8,128)(2,1)S(1)}, bf16[4,2,176,512]{3,2,1,0:T(8,128)(2,1)}, bf16[4,2,176,512]{3...) custom-call(s32[3]{0:T(128)S(1)} %pad_add_fusion.place_ref, ...), custom_call_target="tpu_custom_call" | custom-call | flops 1 | bytes 27262976 | tf_op jit(solution)/shard_map/fold/pallas_call | solution.py:656
  296.5 9.0 %weight_grads.2 = (bf16[2,2,4,128,512]{4,3,2,1,0:T(8,128)(2,1)S(1)}, bf16[2,2,4,128,512]{4,3,2,1,0:T(8,128)(2,1)}) custom-call(s32[1]{0:T(128)} %bitcast.core_ref, bf16[1024,1024]{1,0:T(8,128)(2,1)S(1)} %copy-done.3, bf16[1024,1024]{1,0:T(8,128)(2,1)S(1)} %copy-done.3, bf16[1024,1024]{1,0:T(8,128)(2,1)S(1)} %copy-done.6, bf16[1024,1024]{1,0:T(8,128)(2,1)S(1)} %copy-done.6, ...), custom_call_target="tpu_custom_call" | custom-call | flops 1 | bytes 1 | tf_op jit(solution)/shard_map/weight_grads/pallas_call | solution.py:544
  316.0 24.5 %attend_back.1 = (bf16[1024,512]{1,0:T(8,128)(2,1)S(1)}, bf16[1024,512]{1,0:T(8,128)(2,1)S(1)}, bf16[1024,1024]{1,0:T(8,128)(2,1)S(1)}, f32[1024,512]{1,0:T(8,128)S(1)}) custom-call(s32[1024]{0:T(1024)S(1)} %bitcast.232, bf16[1024,512]{1,0:T(8,128)(2,1)S(1)} %copy-done.28, bf16[1024,512]{1,0:T(8,128)(2,1)S(1)} %copy-done.30, ...), custom_call_target="tpu_custom_call" | custom-call | flops 1 | bytes 1 | tf_op jit(solution)/shard_map/attend_back/pallas_call | solution.py:261
  342.0 10.9 %weight_grads.3 = (bf16[2,2,4,128,512]{4,3,2,1,0:T(8,128)(2,1)S(1)}, bf16[2,2,4,128,512]{4,3,2,1,0:T(8,128)(2,1)}) custom-call(s32[1]{0:T(128)} %bitcast.core_ref, bf16[1024,1024]{1,0:T(8,128)(2,1)S(1)} %copy-done.3, bf16[1024,1024]{1,0:T(8,128)(2,1)S(1)} %copy-done.3, bf16[1024,512]{1,0:T(8,128)(2,1)S(1)} %get-tuple-element.138.refs_2_.gq_ref, ...), custom_call_target="tpu_custom_call" | custom-call | flops 1 | bytes 1 | tf_op jit(solution)/shard_map/weight_grads/pallas_call | solution.py:544
  379.2 20.9 %unproject.1 = (f32[1024,1024]{1,0:T(8,128)}, f32[16,1024]{1,0:T(8,128)}, f32[16,512]{1,0:T(8,128)}, f32[1,512]{1,0:T(1,128)}, f32[1,1024]{1,0:T(1,128)}) custom-call(bf16[1024,1024]{1,0:T(8,128)(2,1)} %x_ref.5, bf16[1024,1024]{1,0:T(8,128)(2,1)} %copy-done.2, bf16[1024,512]{1,0:T(8,128)(2,1)} %copy-done.11, bf16[1024,512]{1,0:T(8,128)(2,1)} %copy-done.12, ...), custom_call_target="tpu_custom_call" | custom-call | flops 6442450944 | bytes 104857600 | tf_op jit(solution)/shard_map/unproject/pallas_call | solution.py:597
  402.5 4.1 collective-permute-done.20
  422.6 13.4 %collective-permute-done.24 = f32[2,4,16,512]{3,2,1,0:T(8,128)S(1)} collective-permute-done((f32[2,4,16,512]{3,2,1,0:T(8,128)S(1)}, f32[2,4,16,512]{3,2,1,0:T(8,128)S(1)}, u32[]{:S(2)}, u32[]{:S(2)}) %collective-permute-start.24) | collective-permute-done | bytes 262176 | tf_op jit(solution)/shard_map/ppermute | solution.py:699
  452.9 7.5 %collective-permute-start.37 = (bf16[176,512]{1,0:T(8,128)(2,1)S(1)}, bf16[176,512]{1,0:T(8,128)(2,1)S(1)}, u32[]{:S(2)}, u32[]{:S(2)}) collective-permute-start(bf16[176,512]{1,0:T(8,128)(2,1)S(1)} %fusion.44), channel_id=1, source_target_pairs={{0,4},{4,0},{1,5},{5,1},{2,6},{6,2},{3,7},{7,3},{8,12},{12,8},{9,1... | collective-permute-start | bytes 540680 | tf_op jit(solution)/shard_map/ppermute | solution.py:699
  463.8 5.6 %collective-permute-done.32 = bf16[128,1024]{1,0:T(8,128)(2,1)S(1)} collective-permute-done((bf16[128,1024]{1,0:T(8,128)(2,1)S(1)}, bf16[128,1024]{1,0:T(8,128)(2,1)S(1)}, u32[]{:S(2)}, u32[]{:S(2)}) %collective-permute-start.32) | collective-permute-done | bytes 262176 | tf_op jit(solution)/shard_map/ppermute | solution.py:714
  472.7 5.5 %collective-permute-done.34 = bf16[128,1024]{1,0:T(8,128)(2,1)S(1)} collective-permute-done((bf16[128,1024]{1,0:T(8,128)(2,1)S(1)}, bf16[128,1024]{1,0:T(8,128)(2,1)S(1)}, u32[]{:S(2)}, u32[]{:S(2)}) %collective-permute-start.34) | collective-permute-done | bytes 262176 | tf_op jit(solution)/shard_map/ppermute | solution.py:682
  480.7 9.1 %collective-permute-done.40 = bf16[176,1536]{1,0:T(8,128)(2,1)S(1)} collective-permute-done((bf16[176,1536]{1,0:T(8,128)(2,1)S(1)}, bf16[176,1536]{1,0:T(8,128)(2,1)S(1)}, u32[]{:S(2)}, u32[]{:S(2)}) %collective-permute-start.40) | collective-permute-done | bytes 540704 | tf_op jit(solution)/shard_map/ppermute | solution.py:682
  (315 shorter events, 142.1 us)
Async XLA Ops:
  7.3 177.1 %all-gather.2.cloned.1.call-start = ((), (), s32[]{:S(2)}) async-start(), calls=%async_computation | async-start | bytes 17842176 | tf_op jit(solution)/shard_map/all_gather | solution.py:772
  42.9 31.1 %collective-permute-start.3 = (bf16[4,272,512]{2,1,0:T(8,128)(2,1)S(1)}, bf16[4,272,512]{2,1,0:T(8,128)(2,1)S(1)}, u32[]{:S(2)}, u32[]{:S(2)}) collective-permute-start(bf16[4,272,512]{2,1,0:T(8,128)(2,1)S(1)} %bitcast_dynamic-update-slice_fusion.14), channel_id=1, source_target_pairs={{0,4},{4,0},{1,5},{5,1},{2,6},{6,2},{3,7},{7,3},{8,12},{12,8},{9,1... | collective-permute-start | bytes 3342344 | tf_op jit(solution)/shard_map/ppermute | solution.py:682
  80.3 24.2 %collective-permute-start.5 = (bf16[256,512]{1,0:T(8,128)(2,1)S(1)}, bf16[256,512]{1,0:T(8,128)(2,1)S(1)}, u32[]{:S(2)}, u32[]{:S(2)}) collective-permute-start(bf16[256,512]{1,0:T(8,128)(2,1)S(1)} %fusion.31), channel_id=1, source_target_pairs={{0,1},{1,2},{2,3},{3,0},{4,5},{5,6},{6,7},{7,4},{8,9},{9,10},{10,1... | collective-permute-start | bytes 786440 | tf_op jit(solution)/shard_map/ppermute | solution.py:714
  80.3 39.1 %collective-permute-start.6 = (bf16[256,512]{1,0:T(8,128)(2,1)S(1)}, bf16[256,512]{1,0:T(8,128)(2,1)}, u32[]{:S(2)}, u32[]{:S(2)}) collective-permute-start(bf16[256,512]{1,0:T(8,128)(2,1)S(1)} %fusion.31), channel_id=1, source_target_pairs={{0,2},{1,3},{2,0},{3,1},{4,6},{5,7},{6,4},{7,5},{8,10},{9,11},{10,... | collective-permute-start | bytes 786440 | tf_op jit(solution)/shard_map/ppermute | solution.py:714
  85.5 48.0 %collective-permute-start.7 = (bf16[256,512]{1,0:T(8,128)(2,1)S(1)}, bf16[256,512]{1,0:T(8,128)(2,1)}, u32[]{:S(2)}, u32[]{:S(2)}) collective-permute-start(bf16[256,512]{1,0:T(8,128)(2,1)S(1)} %fusion.31), channel_id=1, source_target_pairs={{0,3},{1,0},{2,1},{3,2},{4,7},{5,4},{6,5},{7,6},{8,11},{9,8},{10,9... | collective-permute-start | bytes 786440 | tf_op jit(solution)/shard_map/ppermute | solution.py:714
  135.6 23.2 %collective-permute-start.8 = (bf16[4,256,512]{2,1,0:T(8,128)(2,1)S(1)}, bf16[4,256,512]{2,1,0:T(8,128)(2,1)S(1)}, u32[]{:S(2)}, u32[]{:S(2)}) collective-permute-start(bf16[4,256,512]{2,1,0:T(8,128)(2,1)S(1)} %bitcast_dynamic-update-slice_fusion.20), channel_id=1, source_target_pairs={{0,4},{4,0},{1,5},{5,1},{2,6},{6,2},{3,7},{7,3},{8,12},{12,8},{9,1... | collective-permute-start | bytes 3145736 | tf_op jit(solution)/shard_map/ppermute | solution.py:699
  291.9 63.0 %collective-permute-start.12 = (bf16[4,2,176,512]{3,2,1,0:T(8,128)(2,1)}, bf16[4,2,176,512]{3,2,1,0:T(8,128)(2,1)}, u32[]{:S(2)}, u32[]{:S(2)}) collective-permute-start(bf16[4,2,176,512]{3,2,1,0:T(8,128)(2,1)} %get-tuple-element.145), channel_id=1, source_target_pairs={{0,16},{16,0},{1,17},{17,1},{2,18},{18,2},{3,19},{19,3},{4,20},{20... | collective-permute-start | bytes 4325384 | tf_op jit(solution)/shard_map/ppermute | solution.py:699
  292.2 62.7 %collective-permute-start.13 = (bf16[4,2,176,512]{3,2,1,0:T(8,128)(2,1)}, bf16[4,2,176,512]{3,2,1,0:T(8,128)(2,1)}, u32[]{:S(2)}, u32[]{:S(2)}) collective-permute-start(bf16[4,2,176,512]{3,2,1,0:T(8,128)(2,1)} %get-tuple-element.146), channel_id=1, source_target_pairs={{0,4},{4,0},{1,5},{5,1},{2,6},{6,2},{3,7},{7,3},{8,12},{12,8},{9,1... | collective-permute-start | bytes 4325384 | tf_op jit(solution)/shard_map/ppermute | solution.py:699
  293.4 61.5 %collective-permute-start.15 = (bf16[2,2,2,176,256]{4,3,2,1,0:T(8,128)(2,1)}, bf16[2,2,2,176,256]{4,3,2,1,0:T(8,128)(2,1)}, u32[]{:S(2)}, u32[]{:S(2)}) collective-permute-start(bf16[2,2,2,176,256]{4,3,2,1,0:T(8,128)(2,1)} %get-tuple-element.148), channel_id=1, source_target_pairs={{0,2},{1,3},{2,0},{3,1},{4,6},{5,7},{6,4},{7,5},{8,10},{9,11},{10,... | collective-permute-start | bytes 2162696 | tf_op jit(solution)/shard_map/ppermute | solution.py:714
  293.4 61.5 %collective-permute-start.16 = (bf16[2,2,2,176,256]{4,3,2,1,0:T(8,128)(2,1)}, bf16[2,2,2,176,256]{4,3,2,1,0:T(8,128)(2,1)}, u32[]{:S(2)}, u32[]{:S(2)}) collective-permute-start(bf16[2,2,2,176,256]{4,3,2,1,0:T(8,128)(2,1)} %get-tuple-element.149), channel_id=1, source_target_pairs={{0,3},{1,0},{2,1},{3,2},{4,7},{5,4},{6,5},{7,6},{8,11},{9,8},{10,9... | collective-permute-start | bytes 2162696 | tf_op jit(solution)/shard_map/ppermute | solution.py:714
  310.4 55.6 %collective-permute-start.18 = (bf16[2,2,4,128,512]{4,3,2,1,0:T(8,128)(2,1)}, bf16[2,2,4,128,512]{4,3,2,1,0:T(8,128)(2,1)}, u32[]{:S(2)}, u32[]{:S(2)}) collective-permute-start(bf16[2,2,4,128,512]{4,3,2,1,0:T(8,128)(2,1)} %get-tuple-element.159), channel_id=1, source_target_pairs={{0,8},{8,0},{1,9},{9,1},{2,10},{10,2},{3,11},{11,3},{4,12},{12,4},... | collective-permute-start | bytes 6291464 | tf_op jit(solution)/shard_map/ppermute | solution.py:699
  373.9 33.5 %collective-permute-start.19 = (bf16[2,4,176,512]{3,2,1,0:T(8,128)(2,1)}, bf16[2,4,176,512]{3,2,1,0:T(8,128)(2,1)}, u32[]{:S(2)}, u32[]{:S(2)}) collective-permute-start(bf16[2,4,176,512]{3,2,1,0:T(8,128)(2,1)} %fusion), channel_id=1, source_target_pairs={{0,1},{1,0},{2,3},{3,2},{4,5},{5,4},{6,7},{7,6},{8,9},{9,8},{10,11... | collective-permute-start | bytes 4325384 | tf_op jit(solution)/shard_map/ppermute | solution.py:699
  373.9 32.7 %collective-permute-start.21 = (bf16[2,4,128,512]{3,2,1,0:T(8,128)(2,1)}, bf16[2,4,128,512]{3,2,1,0:T(8,128)(2,1)}, u32[]{:S(2)}, u32[]{:S(2)}) collective-permute-start(bf16[2,4,128,512]{3,2,1,0:T(8,128)(2,1)} %get-tuple-element.167), channel_id=1, source_target_pairs={{0,4},{4,0},{1,5},{5,1},{2,6},{6,2},{3,7},{7,3},{8,12},{12,8},{9,1... | collective-permute-start | bytes 3145736 | tf_op jit(solution)/shard_map/ppermute | solution.py:699
  374.1 32.5 %collective-permute-start.22 = (bf16[2,4,128,512]{3,2,1,0:T(8,128)(2,1)}, bf16[2,4,128,512]{3,2,1,0:T(8,128)(2,1)}, u32[]{:S(2)}, u32[]{:S(2)}) collective-permute-start(bf16[2,4,128,512]{3,2,1,0:T(8,128)(2,1)} %get-tuple-element.168), channel_id=1, source_target_pairs={{0,16},{16,0},{1,17},{17,1},{2,18},{18,2},{3,19},{19,3},{4,20},{20... | collective-permute-start | bytes 3145736 | tf_op jit(solution)/shard_map/ppermute | solution.py:699
  378.9 27.7 %collective-permute-start.20 = (bf16[2,2,176,256]{3,2,1,0:T(8,128)(2,1)S(1)}, bf16[2,2,176,256]{3,2,1,0:T(8,128)(2,1)S(1)}, u32[]{:S(2)}, u32[]{:S(2)}) collective-permute-start(bf16[2,2,176,256]{3,2,1,0:T(8,128)(2,1)S(1)} %get-tuple-element.166), channel_id=1, source_target_pairs={{0,16},{16,0},{1,17},{17,1},{2,18},{18,2},{3,19},{19,3},{4,20},{20... | collective-permute-start | bytes 1081352 | tf_op jit(solution)/shard_map/ppermute | solution.py:699
  411.8 41.0 %collective-permute-start.36 = (bf16[4,176,512]{2,1,0:T(8,128)(2,1)S(1)}, bf16[4,176,512]{2,1,0:T(8,128)(2,1)S(1)}, u32[]{:S(2)}, u32[]{:S(2)}) collective-permute-start(bf16[4,176,512]{2,1,0:T(8,128)(2,1)S(1)} %get-tuple-element.182), channel_id=1, source_target_pairs={{0,2},{1,3},{2,0},{3,1},{4,6},{5,7},{6,4},{7,5},{8,10},{9,11},{10,... | collective-permute-start | bytes 2162696 | tf_op jit(solution)/shard_map/ppermute | solution.py:699
  417.2 19.6 %collective-permute-start.30 = (bf16[4,128,512]{2,1,0:T(8,128)(2,1)S(1)}, bf16[4,128,512]{2,1,0:T(8,128)(2,1)S(1)}, u32[]{:S(2)}, u32[]{:S(2)}) collective-permute-start(bf16[4,128,512]{2,1,0:T(8,128)(2,1)S(1)} %fusion.13), channel_id=1, source_target_pairs={{0,16},{16,0},{1,17},{17,1},{2,18},{18,2},{3,19},{19,3},{4,20},{20... | collective-permute-start | bytes 1572872 | tf_op jit(solution)/shard_map/ppermute | solution.py:699
  417.8 20.2 %collective-permute-start.29 = (bf16[4,128,512]{2,1,0:T(8,128)(2,1)S(1)}, bf16[4,128,512]{2,1,0:T(8,128)(2,1)S(1)}, u32[]{:S(2)}, u32[]{:S(2)}) collective-permute-start(bf16[4,128,512]{2,1,0:T(8,128)(2,1)S(1)} %fusion.12), channel_id=1, source_target_pairs={{0,4},{4,0},{1,5},{5,1},{2,6},{6,2},{3,7},{7,3},{8,12},{12,8},{9,1... | collective-permute-start | bytes 1572872 | tf_op jit(solution)/shard_map/ppermute | solution.py:699
  418.8 17.2 %collective-permute-start.24 = (f32[2,4,16,512]{3,2,1,0:T(8,128)S(1)}, f32[2,4,16,512]{3,2,1,0:T(8,128)S(1)}, u32[]{:S(2)}, u32[]{:S(2)}) collective-permute-start(f32[2,4,16,512]{3,2,1,0:T(8,128)S(1)} %fusion.70), channel_id=1, source_target_pairs={{0,16},{16,0},{1,17},{17,1},{2,18},{18,2},{3,19},{19,3},{4,20},{20... | collective-permute-start | bytes 786440 | tf_op jit(solution)/shard_map/ppermute | solution.py:699
  443.3 20.5 %collective-permute-start.31 = (bf16[128,1024]{1,0:T(8,128)(2,1)S(1)}, bf16[128,1024]{1,0:T(8,128)(2,1)S(1)}, u32[]{:S(2)}, u32[]{:S(2)}) collective-permute-start(bf16[128,1024]{1,0:T(8,128)(2,1)S(1)} %get-tuple-element.200), channel_id=1, source_target_pairs={{0,1},{1,2},{2,3},{3,0},{4,5},{5,6},{6,7},{7,4},{8,9},{9,10},{10,1... | collective-permute-start | bytes 786440 | tf_op jit(solution)/shard_map/ppermute | solution.py:714
  447.0 22.4 %collective-permute-start.32 = (bf16[128,1024]{1,0:T(8,128)(2,1)S(1)}, bf16[128,1024]{1,0:T(8,128)(2,1)S(1)}, u32[]{:S(2)}, u32[]{:S(2)}) collective-permute-start(bf16[128,1024]{1,0:T(8,128)(2,1)S(1)} %get-tuple-element.201), channel_id=1, source_target_pairs={{0,2},{1,3},{2,0},{3,1},{4,6},{5,7},{6,4},{7,5},{8,10},{9,11},{10,... | collective-permute-start | bytes 786440 | tf_op jit(solution)/shard_map/ppermute | solution.py:714
  447.3 23.2 %collective-permute-start.33 = (bf16[128,1024]{1,0:T(8,128)(2,1)S(1)}, bf16[128,1024]{1,0:T(8,128)(2,1)S(1)}, u32[]{:S(2)}, u32[]{:S(2)}) collective-permute-start(bf16[128,1024]{1,0:T(8,128)(2,1)S(1)} %get-tuple-element.202), channel_id=1, source_target_pairs={{0,3},{1,0},{2,1},{3,2},{4,7},{5,4},{6,5},{7,6},{8,11},{9,8},{10,9... | collective-permute-start | bytes 786440 | tf_op jit(solution)/shard_map/ppermute | solution.py:714
  452.9 18.5 %collective-permute-start.37 = (bf16[176,512]{1,0:T(8,128)(2,1)S(1)}, bf16[176,512]{1,0:T(8,128)(2,1)S(1)}, u32[]{:S(2)}, u32[]{:S(2)}) collective-permute-start(bf16[176,512]{1,0:T(8,128)(2,1)S(1)} %fusion.44), channel_id=1, source_target_pairs={{0,4},{4,0},{1,5},{5,1},{2,6},{6,2},{3,7},{7,3},{8,12},{12,8},{9,1... | collective-permute-start | bytes 540680 | tf_op jit(solution)/shard_map/ppermute | solution.py:699
  471.7 18.1 %collective-permute-start.40 = (bf16[176,1536]{1,0:T(8,128)(2,1)S(1)}, bf16[176,1536]{1,0:T(8,128)(2,1)S(1)}, u32[]{:S(2)}, u32[]{:S(2)}) collective-permute-start(bf16[176,1536]{1,0:T(8,128)(2,1)S(1)} %pad_maximum_fusion.4), channel_id=1, source_target_pairs={{0,16},{16,0},{1,17},{17,1},{2,18},{18,2},{3,19},{19,3},{4,20},{20... | collective-permute-start | bytes 1622024 | tf_op jit(solution)/shard_map/ppermute | solution.py:682
  (82 other events, 878.0 us)
Sparse Core Ops, SparseCore 0:
  11.6 141.0 all-gather.1
